TPU v7x, 256 devices: a whole 4x4x8 slice. The times are simulated.
256 devices in a mesh: leaf: 128 (over x, y, z), rhs: 2 (over core).
Axes of the slice: x: 4, y: 4, z: 8, core: 2. Of those that a mesh axis runs over, the one named last changes fastest.
Arguments:
- right_sides: float32 [16, 262144], P('rhs', 'leaf'), may hold values from -6 to 6
- point_order: int32 [262144], P('leaf'), may hold values from 0 to 262143, as said below
- leaf_basis: bfloat16 [2048, 64, 128], P('leaf'), may hold values from -0.5 to 0.5
- transfer: bfloat16 [1920, 64, 128], P('leaf'), may hold values from -0.5 to 0.5
- coupling: bfloat16 [3968, 64, 512], P('leaf'), may hold values from -0.25 to 0.25
- far_list: int32 [3968, 8], P('leaf'), may hold values from 0 to 2047, as said below
- far_count: int32 [3968], P('leaf'), may hold values from 0 to 8
- coarse_transfer: bfloat16 [96, 64, 128], replicated, may hold values from -0.5 to 0.5
- coarse_coupling: bfloat16 [96, 64, 192], replicated, may hold values from -0.4375 to 0.4375
- coarse_list: int32 [96, 3], replicated, may hold values from 0 to 63, as said below
- coarse_count: int32 [96], replicated, may hold values from 0 to 3
- near_block: bfloat16 [2048, 28, 128, 128], P('leaf', 'rhs'), may hold values from -0.125 to 0.125
- near_list: int32 [2048, 28], P('leaf', 'rhs'), may hold values from 0 to 2047, as said below
- near_count: int32 [2048], P('leaf'), may hold values from 1 to 27
Outputs:
- product: float32 [16, 262144], P('rhs', 'leaf')
Inputs may be any that keep to these rules, and one draw needn't show every extreme that they name: `point_order`: each aligned block of 2048 entries is a permutation of that block's own positions. `far_list`: leaf j is the cell (j // 16, y, z) of a grid of 128 x 4 x 4 cells, y taken from the even and z from the odd bits of j mod 16; a node is the box of its leaves. Slots below far_count of node j at level h <= D (w nodes a block) hold distinct nodes of level h whose boxes do not touch node j's box while their parents' boxes touch or equal the parent's box; every entry equals j + k with |k| <= 3 w; unused slots hold j. `coarse_list`: slots below coarse_count of node j at level D + g hold distinct nodes of that level equal to j + k with 2 <= |k| <= 3 and parents at most one step from j's parent; unused slots hold j. `near_list`: slot 0 of leaf j is j; slots 1 to near_count - 1 hold distinct other leaves whose cells touch leaf j's cell in the grid described for far_list; later slots hold j.
All inputs are finite; a program needn't handle non-finite values.
Results may differ from a plain program's by a relative error of at most 0.017.
Values may be sent and summed in bfloat16 or wider, within the bound.
A program may use at most 128 MiB of HBM per device.

v0:
```python
import jax
import jax.numpy as jnp
import numpy as np
from jax import lax
from jax.sharding import PartitionSpec as P

REACH = 3
COARSE_REACH = 3
TOP = 2


def from_behind(shard, axis, by):
    devices = lax.axis_size(axis)
    return lax.ppermute(shard, axis, [(i, (i + by) % devices) for i in range(devices)])


def partner(value, axis, distance):
    mask = 2**distance
    pairs = [(source, source ^ mask) for source in range(lax.axis_size(axis))]
    return lax.ppermute(value, axis, pairs)


def lift_terms(matrices, vectors):
    return jnp.einsum("nab,rnb->rna", matrices, vectors, preferred_element_type=jnp.float32)


def lower_terms(matrices, vectors):
    return jnp.einsum("nab,rna->rnb", matrices, vectors, preferred_element_type=jnp.float32)


def couple_far(matrices, window, slot_ids, counts):
    live_mask = jnp.arange(slot_ids.shape[1])[None, :] < counts[:, None]
    picked = window[:, slot_ids] * live_mask[None, :, :, None].astype(window.dtype)
    picked = picked.reshape(window.shape[0], slot_ids.shape[0], slot_ids.shape[1] * window.shape[2])
    return lift_terms(matrices, picked)


def near_terms(window, near_blocks, slot_ids, live_mask):
    picked = window[:, slot_ids] * live_mask[None, :, :, None].astype(window.dtype)
    return jnp.einsum("jsab,rjsb->rja", near_blocks, picked, preferred_element_type=jnp.float32)


def body(
    right_sides,
    point_order,
    leaf_basis,
    transfer,
    coupling,
    far_list,
    far_count,
    coarse_transfer,
    coarse_coupling,
    coarse_list,
    coarse_count,
    near_block,
    near_list,
    near_count,
):
    rhs_local, own_points = right_sides.shape
    leaf_count, rank_size, leaf_size = leaf_basis.shape
    tree_depth = leaf_count.bit_length() - 1
    devices = lax.axis_size("leaf")
    my_place = lax.axis_index("leaf")
    points = jnp.take(right_sides, point_order - my_place * own_points, axis=1).astype(jnp.bfloat16)
    coeffs = [
        lift_terms(leaf_basis, points.reshape(rhs_local, leaf_count, leaf_size)).astype(
            jnp.bfloat16
        )
    ]
    for height in range(1, tree_depth + 1):
        node_width = leaf_count >> height
        matrices = transfer[leaf_count - 2 * node_width : leaf_count - node_width]
        coeffs.append(
            lift_terms(matrices, coeffs[-1].reshape(rhs_local, node_width, 2 * rank_size)).astype(
                jnp.bfloat16
            )
        )
    packed = jnp.concatenate(coeffs, axis=1)
    pack_rows = packed.shape[1]
    beside_all = []
    for offset in range(-REACH, REACH + 1):
        if offset == 0:
            beside_all.append(packed)
        else:
            beside_all.append(from_behind(packed, "leaf", -offset))
    far_window = jnp.concatenate(beside_all, axis=1)
    row_width = np.concatenate(
        [
            np.full(leaf_count >> height, leaf_count >> height, dtype=np.int32)
            for height in range(tree_depth + 1)
        ]
    )
    row_first = np.concatenate(
        [
            np.full(
                leaf_count >> height, 2 * leaf_count - 2 * (leaf_count >> height), dtype=np.int32
            )
            for height in range(tree_depth + 1)
        ]
    )
    owner_gap = (far_list // row_width[:, None] - my_place + REACH) % devices
    far_ids = owner_gap * pack_rows + row_first[:, None] + far_list % row_width[:, None]
    far_fields = couple_far(coupling, far_window, far_ids, far_count)
    root_coeff = coeffs[tree_depth]
    chain = [root_coeff]
    chain_mats = [None]
    for height in range(1, TOP + 1):
        sibling = partner(chain[-1], "leaf", height - 1)
        on_left = my_place >> height - 1 & 1 == 0
        paired = jnp.where(
            on_left,
            jnp.concatenate([chain[-1], sibling], 2),
            jnp.concatenate([sibling, chain[-1]], 2),
        )
        node_width = devices >> height
        row_here = devices - 2 * node_width + (my_place >> height)
        matrices = lax.dynamic_slice_in_dim(coarse_transfer, row_here, 1, 0)
        chain_mats.append(matrices)
        chain.append(lift_terms(matrices, paired).astype(jnp.bfloat16))
    field = None
    for height in range(TOP, 0, -1):
        node_width = devices >> height
        node_here = my_place >> height
        row_here = devices - 2 * node_width + node_here
        nearby_nodes = []
        for offset in range(-COARSE_REACH, COARSE_REACH + 1):
            if offset == 0:
                nearby_nodes.append(chain[height])
            else:
                nearby_nodes.append(from_behind(chain[height], "leaf", -offset * 2**height))
        node_window = jnp.concatenate(nearby_nodes, 1)
        partners = lax.dynamic_slice_in_dim(coarse_list, row_here, 1, 0)
        slot_ids = (partners - node_here + COARSE_REACH) % node_width
        counts = lax.dynamic_slice_in_dim(coarse_count, row_here, 1, 0)
        matrices = lax.dynamic_slice_in_dim(coarse_coupling, row_here, 1, 0)
        incoming = couple_far(matrices, node_window, slot_ids, counts)
        if height < TOP:
            halves = lower_terms(chain_mats[height + 1], field)
            side = my_place >> height & 1
            incoming = incoming + lax.dynamic_slice_in_dim(halves, side * rank_size, rank_size, 2)
        field = incoming.astype(jnp.bfloat16)
    halves = lower_terms(chain_mats[1], field)
    from_above = lax.dynamic_slice_in_dim(halves, (my_place & 1) * rank_size, rank_size, 2)
    root_row = 2 * leaf_count - 2
    field = (far_fields[:, root_row : root_row + 1] + from_above).astype(jnp.bfloat16)
    for height in range(tree_depth - 1, -1, -1):
        node_width = leaf_count >> height
        first_row = 2 * leaf_count - 2 * node_width
        matrices = transfer[leaf_count - node_width : leaf_count - node_width // 2]
        down = lower_terms(matrices, field).reshape(rhs_local, node_width, rank_size)
        field = (far_fields[:, first_row : first_row + node_width] + down).astype(jnp.bfloat16)
    far_part = lower_terms(leaf_basis, field).reshape(rhs_local, own_points)
    sides = [from_behind(points, "leaf", by_step) for by_step in (1, -1)]
    nearby = jnp.concatenate([sides[0], points, sides[1]], axis=1)
    whole = lax.all_gather(nearby, "rhs", axis=0, tiled=True)
    window = whole.reshape(whole.shape[0], 3 * leaf_count, leaf_size)
    near_gap = (near_list // leaf_count - my_place + 1) % devices
    near_ids = near_gap * leaf_count + near_list % leaf_count
    slot_base = lax.axis_index("rhs") * near_list.shape[1]
    live_mask = (slot_base + jnp.arange(near_list.shape[1]))[None, :] < near_count[:, None]
    terms = near_terms(window, near_block, near_ids, live_mask)
    near_part = lax.psum_scatter(
        terms.reshape(whole.shape[0], own_points), "rhs", scatter_dimension=0, tiled=True
    )
    return far_part + near_part


def solution(mesh):
    return jax.shard_map(
        body,
        mesh=mesh,
        in_specs=(
            P("rhs", "leaf"),
            P("leaf"),
            P("leaf", None, None),
            P("leaf", None, None),
            P("leaf", None, None),
            P("leaf", None),
            P("leaf"),
            P(),
            P(),
            P(),
            P(),
            P("leaf", "rhs", None, None),
            P("leaf", "rhs"),
            P("leaf"),
        ),
        out_specs=P("rhs", "leaf"),
        check_vma=False,
    )
```

profile of v0, /device:TPU:7, one launch (start us, length us, event | category | flops | bytes accessed | tf_op | source)
XLA Modules:
  0.0 212.6 jit_solution(11111049817826819093)
XLA Ops:
  6.6 0.9 fusion.58
  7.5 0.8 fusion.108
  8.3 1.9 copy.92
  10.1 8.7 %gather_fusion = bf16[2048,8]{1,0:T(8,128)(2,1)} fusion(bf16[8,2048]{0,1:T(8,128)(2,1)} %copy.92, s32[2048]{0:T(1024)S(1)} %fusion.58), kind=kCustom, calls=%fused_computation | custom fusion | bytes 73728 | tf_op jit(solution)/shard_map/jit(_take)/gather | solution.py:64
  18.9 1.2 copy.93
  20.1 1.8 constant_dynamic-update-slice_fusion.4
  22.0 1.7 constant_dynamic-update-slice_fusion.3
  23.8 0.7 constant_dynamic-update-slice_fusion.2
  24.7 0.7 constant_dynamic-update-slice_fusion.1
  25.5 0.7 constant_dynamic-update-slice_fusion
  26.2 4.3 %collective-permute-start = (bf16[8,31,64]{2,0,1:T(8,128)(2,1)}, bf16[8,31,64]{2,0,1:T(8,128)(2,1)}, u32[]{:S(2)}, u32[]{:S(2)}) collective-permute-start(bf16[8,31,64]{2,0,1:T(8,128)(2,1)} %get-tuple-element.17), channel_id=1, source_target_pairs={{0,6},{2,8},{4,10},{6,12},{8,14},{10,16},{12,18},{14,20},{16,22},{... | collective-permute-start | bytes 95240 | tf_op jit(solution)/shard_map/ppermute | solution.py:14
  30.5 3.3 %collective-permute-start.1 = (bf16[8,31,64]{2,0,1:T(8,128)(2,1)}, bf16[8,31,64]{2,0,1:T(8,128)(2,1)}, u32[]{:S(2)}, u32[]{:S(2)}) collective-permute-start(bf16[8,31,64]{2,0,1:T(8,128)(2,1)} %get-tuple-element.17), channel_id=1, source_target_pairs={{0,4},{2,6},{4,8},{6,10},{8,12},{10,14},{12,16},{14,18},{16,20},{1... | collective-permute-start | bytes 95240 | tf_op jit(solution)/shard_map/ppermute | solution.py:14
  33.8 0.7 collective-permute-start.2
  34.6 0.7 collective-permute-start.6
  35.6 1.4 fusion.99
  37.0 0.8 compare_select_fusion.2
  38.0 0.7 fusion.43
  38.8 2.2 %fusion.10 = bf16[8,2048]{0,1:T(8,128)(2,1)} fusion(bf16[2048,8]{1,0:T(8,128)(2,1)} %gather_fusion, pred[2048]{0:T(1024)(128)(4,1)S(1)} %compare_and_fusion), kind=kLoop, calls=%fused_computation.32 | loop fusion | flops 16384 | bytes 67584 | tf_op jit(solution)/shard_map/convert_element_type | solution.py:64
  41.0 0.7 compare_select_fusion
  41.8 1.3 compare_convert_fusion
  43.7 0.9 convolution_convert_fusion.6
  44.6 3.4 %collective-permute-start.7 = (bf16[8,1,64]{2,0,1:T(8,128)(2,1)S(1)}, bf16[8,1,64]{2,0,1:T(8,128)(2,1)S(1)}, u32[]{:S(2)}, u32[]{:S(2)}) collective-permute-start(bf16[8,1,64]{2,0,1:T(8,128)(2,1)S(1)} %bitcast.129), channel_id=1, source_target_pairs={{0,12},{2,14},{4,16},{6,18},{8,20},{10,22},{12,24},{14,26},{16,28}... | collective-permute-start | bytes 3080 | tf_op jit(solution)/shard_map/ppermute | solution.py:14
  48.9 0.7 mul.101
  50.3 1.8 copy.113
  52.1 2.2 %collective-permute-start.8 = (bf16[8,1,64]{2,0,1:T(8,128)(2,1)S(1)}, bf16[8,1,64]{2,0,1:T(8,128)(2,1)S(1)}, u32[]{:S(2)}, u32[]{:S(2)}) collective-permute-start(bf16[8,1,64]{2,0,1:T(8,128)(2,1)S(1)} %bitcast.131), channel_id=1, source_target_pairs={{0,8},{2,10},{4,12},{6,14},{8,16},{10,18},{12,20},{14,22},{16,24},... | collective-permute-start | bytes 3080 | tf_op jit(solution)/shard_map/ppermute | solution.py:14
  54.3 7.2 %collective-permute-done.8 = bf16[8,1,64]{2,0,1:T(8,128)(2,1)S(1)} collective-permute-done((bf16[8,1,64]{2,0,1:T(8,128)(2,1)S(1)}, bf16[8,1,64]{2,0,1:T(8,128)(2,1)S(1)}, u32[]{:S(2)}, u32[]{:S(2)}) %collective-permute-start.8) | collective-permute-done | bytes 1056 | tf_op jit(solution)/shard_map/ppermute | solution.py:14
  61.4 2.4 %collective-permute-start.9 = (bf16[8,1,64]{2,0,1:T(8,128)(2,1)S(1)}, bf16[8,1,64]{2,0,1:T(8,128)(2,1)S(1)}, u32[]{:S(2)}, u32[]{:S(2)}) collective-permute-start(bf16[8,1,64]{2,0,1:T(8,128)(2,1)S(1)} %bitcast.132), channel_id=1, source_target_pairs={{0,4},{2,6},{4,8},{6,10},{8,12},{10,14},{12,16},{14,18},{16,20},{1... | collective-permute-start | bytes 3080 | tf_op jit(solution)/shard_map/ppermute | solution.py:14
  63.8 5.2 %collective-permute-done.9 = bf16[8,1,64]{2,0,1:T(8,128)(2,1)S(1)} collective-permute-done((bf16[8,1,64]{2,0,1:T(8,128)(2,1)S(1)}, bf16[8,1,64]{2,0,1:T(8,128)(2,1)S(1)}, u32[]{:S(2)}, u32[]{:S(2)}) %collective-permute-start.9) | collective-permute-done | bytes 1056 | tf_op jit(solution)/shard_map/ppermute | solution.py:14
  69.0 3.6 %collective-permute-done.10 = bf16[8,1,64]{2,0,1:T(8,128)(2,1)S(1)} collective-permute-done((bf16[8,1,64]{2,0,1:T(8,128)(2,1)S(1)}, bf16[8,1,64]{2,0,1:T(8,128)(2,1)S(1)}, u32[]{:S(2)}, u32[]{:S(2)}) %collective-permute-start.10) | collective-permute-done | bytes 1056 | tf_op jit(solution)/shard_map/ppermute | solution.py:14
  72.6 6.3 %collective-permute-done.11 = bf16[8,1,64]{2,0,1:T(8,128)(2,1)S(1)} collective-permute-done((bf16[8,1,64]{2,0,1:T(8,128)(2,1)S(1)}, bf16[8,1,64]{2,0,1:T(8,128)(2,1)S(1)}, u32[]{:S(2)}, u32[]{:S(2)}) %collective-permute-start.11) | collective-permute-done | bytes 1056 | tf_op jit(solution)/shard_map/ppermute | solution.py:14
  79.6 5.9 %collective-permute-start.3 = (bf16[8,31,64]{2,0,1:T(8,128)(2,1)}, bf16[8,31,64]{2,0,1:T(8,128)(2,1)S(1)}, u32[]{:S(2)}, u32[]{:S(2)}) collective-permute-start(bf16[8,31,64]{2,0,1:T(8,128)(2,1)} %get-tuple-element.17), channel_id=1, source_target_pairs={{0,254},{2,0},{4,2},{6,4},{8,6},{10,8},{12,10},{14,12},{16,14},{18... | collective-permute-start | bytes 95240 | tf_op jit(solution)/shard_map/ppermute | solution.py:14
  85.6 0.9 fusion.7
  87.2 8.9 %collective-permute-done.14 = bf16[8,1,64]{2,0,1:T(8,128)(2,1)S(1)} collective-permute-done((bf16[8,1,64]{2,0,1:T(8,128)(2,1)S(1)}, bf16[8,1,64]{2,0,1:T(8,128)(2,1)S(1)}, u32[]{:S(2)}, u32[]{:S(2)}) %collective-permute-start.14) | collective-permute-done | bytes 1056 | tf_op jit(solution)/shard_map/ppermute | solution.py:14
  96.1 4.8 %collective-permute-done.15 = bf16[8,1,64]{2,0,1:T(8,128)(2,1)S(1)} collective-permute-done((bf16[8,1,64]{2,0,1:T(8,128)(2,1)S(1)}, bf16[8,1,64]{2,0,1:T(8,128)(2,1)S(1)}, u32[]{:S(2)}, u32[]{:S(2)}) %collective-permute-start.15) | collective-permute-done | bytes 1056 | tf_op jit(solution)/shard_map/ppermute | solution.py:14
  100.9 1.9 collective-permute-start.16
  102.8 7.5 %collective-permute-done.16 = bf16[8,1,64]{2,0,1:T(8,128)(2,1)S(1)} collective-permute-done((bf16[8,1,64]{2,0,1:T(8,128)(2,1)S(1)}, bf16[8,1,64]{2,0,1:T(8,128)(2,1)S(1)}, u32[]{:S(2)}, u32[]{:S(2)}) %collective-permute-start.16) | collective-permute-done | bytes 1056 | tf_op jit(solution)/shard_map/ppermute | solution.py:14
  110.3 6.3 %collective-permute-done.17 = bf16[8,1,64]{2,0,1:T(8,128)(2,1)S(1)} collective-permute-done((bf16[8,1,64]{2,0,1:T(8,128)(2,1)S(1)}, bf16[8,1,64]{2,0,1:T(8,128)(2,1)S(1)}, u32[]{:S(2)}, u32[]{:S(2)}) %collective-permute-start.17) | collective-permute-done | bytes 1056 | tf_op jit(solution)/shard_map/ppermute | solution.py:14
  116.7 2.7 %collective-permute-done.18 = bf16[8,1,64]{2,0,1:T(8,128)(2,1)S(1)} collective-permute-done((bf16[8,1,64]{2,0,1:T(8,128)(2,1)S(1)}, bf16[8,1,64]{2,0,1:T(8,128)(2,1)S(1)}, u32[]{:S(2)}, u32[]{:S(2)}) %collective-permute-start.18) | collective-permute-done | bytes 1056 | tf_op jit(solution)/shard_map/ppermute | solution.py:14
  119.4 2.4 %collective-permute-start.19 = (bf16[8,1,64]{2,0,1:T(8,128)(2,1)S(1)}, bf16[8,1,64]{2,0,1:T(8,128)(2,1)S(1)}, u32[]{:S(2)}, u32[]{:S(2)}) collective-permute-start(bf16[8,1,64]{2,0,1:T(8,128)(2,1)S(1)} %fusion.7), channel_id=1, source_target_pairs={{0,232},{2,234},{4,236},{6,238},{8,240},{10,242},{12,244},{14,246}... | collective-permute-start | bytes 3080 | tf_op jit(solution)/shard_map/ppermute | solution.py:14
  121.8 4.8 %collective-permute-done.19 = bf16[8,1,64]{2,0,1:T(8,128)(2,1)S(1)} collective-permute-done((bf16[8,1,64]{2,0,1:T(8,128)(2,1)S(1)}, bf16[8,1,64]{2,0,1:T(8,128)(2,1)S(1)}, u32[]{:S(2)}, u32[]{:S(2)}) %collective-permute-start.19) | collective-permute-done | bytes 1056 | tf_op jit(solution)/shard_map/ppermute | solution.py:14
  126.6 5.4 %collective-permute-start.4 = (bf16[8,31,64]{2,0,1:T(8,128)(2,1)}, bf16[8,31,64]{2,0,1:T(8,128)(2,1)S(1)}, u32[]{:S(2)}, u32[]{:S(2)}) collective-permute-start(bf16[8,31,64]{2,0,1:T(8,128)(2,1)} %get-tuple-element.17), channel_id=1, source_target_pairs={{0,252},{2,254},{4,0},{6,2},{8,4},{10,6},{12,8},{14,10},{16,12},{1... | collective-permute-start | bytes 95240 | tf_op jit(solution)/shard_map/ppermute | solution.py:14
  132.8 1.0 fusion.8
  133.7 1.6 fusion.9
  135.7 1.5 constant_dynamic-update-slice_fusion.15
  137.2 2.8 %collective-permute-start.20 = (bf16[8,2048]{0,1:T(8,128)(2,1)}, bf16[8,2048]{0,1:T(8,128)(2,1)}, u32[]{:S(2)}, u32[]{:S(2)}) collective-permute-start(bf16[8,2048]{0,1:T(8,128)(2,1)} %fusion.10), channel_id=1, source_target_pairs={{0,2},{2,4},{4,6},{6,8},{8,10},{10,12},{12,14},{14,16},{16,18},{18... | collective-permute-start | bytes 98312 | tf_op jit(solution)/shard_map/ppermute | solution.py:14
  140.1 1.5 constant_dynamic-update-slice_fusion.14
  141.5 2.8 %collective-permute-start.21 = (bf16[8,2048]{0,1:T(8,128)(2,1)}, bf16[8,2048]{0,1:T(8,128)(2,1)}, u32[]{:S(2)}, u32[]{:S(2)}) collective-permute-start(bf16[8,2048]{0,1:T(8,128)(2,1)} %fusion.10), channel_id=1, source_target_pairs={{0,254},{2,0},{4,2},{6,4},{8,6},{10,8},{12,10},{14,12},{16,14},{18... | collective-permute-start | bytes 98312 | tf_op jit(solution)/shard_map/ppermute | solution.py:14
  147.4 1.2 constant_dynamic-update-slice_fusion.8
  150.5 2.6 %gather_fusion.1 = bf16[248,8,64]{2,1,0:T(8,128)(2,1)} fusion(bf16[8,217,64]{2,0,1:T(8,128)(2,1)} %constant_dynamic-update-slice_fusion.5, s32[1024]{0:T(1024)S(1)} %pad_clamp_fusion.3), kind=kCustom, calls=%fused_computation.1 | custom fusion | bytes 508896 | tf_op jit(solution)/shard_map/gather | solution.py:33
  153.1 1.9 copy.102
  155.0 1.4 gather.23
  156.4 2.2 %convolution_bitcast_fusion.2 = f32[8,31,64]{2,0,1:T(8,128)S(1)} fusion(bf16[31,64,512]{2,1,0:T(8,128)(2,1)} %param.21, bf16[8,31,512]{2,0,1:T(8,128)(2,1)S(1)} %gather.23, bf16[31,512]{1,0:T(8,128)(2,1)} %mul.101), kind=kOutput, calls=%fused_computation.8 | convolution fusion | flops 16379904 | bytes 2380800 | tf_op jit(solution)/shard_map/nab,rnb->rna/dot_general | solution.py:24
  158.6 1.1 convolution_bitcast_fusion.5
  159.8 1.2 copy.112
  161.0 1.2 copy.114
  162.2 0.8 pad_maximum_fusion
  163.0 16.5 %all_gather.3 = bf16[16,6144]{1,0:T(8,128)(2,1)S(1)} all-gather(bf16[8,6144]{1,0:T(8,128)(2,1)S(1)} %pad_maximum_fusion), channel_id=1, replica_groups=mesh['leaf'=128,'rhs'=2] {'rhs'}, dimensions={0}, use_global_device_ids=true | all-gather | bytes 294912 | tf_op jit(solution)/shard_map/all_gather | solution.py:155
  179.5 1.7 gather_fusion.4
  181.2 5.5 %convolution_bitcast_fusion.1 = f32[16,2,8,128]{3,2,1,0:T(8,128)S(1)} fusion(bf16[16,14,128,128]{3,2,1,0:T(8,128)(2,1)} %param.28, bf16[16,14,16,128]{3,2,1,0:T(8,128)(2,1)} %bitcast.124, bf16[16,14]{1,0:T(8,128)(2,1)} %compare_convert_fusion), kind=kOutput, calls=%fused_computation.7 | convolution fusion | flops 117899264 | bytes 8389056 | tf_op jit(solution)/shard_map/jsab,rjsb->rja/dot_general | solution.py:40
  187.4 1.0 convolution_bitcast_fusion.4
  189.1 1.1 convolution_bitcast_fusion.3
  190.8 1.5 reshape.332
  192.2 11.8 %reduce-scatter.2.cloned.1.call-done = f32[8,2048]{1,0:T(8,128)} async-done(((f32[16,2048]{1,0:T(8,128)}), f32[8,2048]{1,0:T(8,128)}) %reduce-scatter.2.cloned.1.call-update) | async-done | bytes 65552 | tf_op jit(solution)/shard_map/reduce_scatter | solution.py:162
  204.0 1.7 fusion
  (95 shorter events, 12.8 us)
Async XLA Ops:
  6.5 126.2 %copy-start = (bf16[96,64,192]{2,1,0:T(8,128)(2,1)S(1)}, bf16[96,64,192]{2,1,0:T(8,128)(2,1)}, u32[]{:S(2)}) copy-start(bf16[96,64,192]{2,1,0:T(8,128)(2,1)} %param.25) | copy-start | bytes 7077892
  6.5 28.8 %copy-start.3 = (s32[2048]{0:T(1024)S(1)}, s32[2048]{0:T(1024)}, u32[]{:S(2)}) copy-start(s32[2048]{0:T(1024)} %param.18) | copy-start | bytes 24580
  6.5 17.3 %copy-start.2 = (bf16[15,64,128]{2,1,0:T(8,128)(2,1)S(1)}, bf16[15,64,128]{2,1,0:T(8,128)(2,1)}, u32[]{:S(2)}) copy-start(bf16[15,64,128]{2,1,0:T(8,128)(2,1)} %param.20) | copy-start | bytes 737284
  6.5 28.8 %copy-start.5 = (s32[96,3]{0,1:T(4,128)S(1)}, s32[96,3]{0,1:T(4,128)}, u32[]{:S(2)}) copy-start(s32[96,3]{0,1:T(4,128)} %param.26) | copy-start | bytes 3460
  6.5 197.5 %reduce-scatter.2.cloned.1.call-start = ((), (), s32[]{:S(2)}) async-start(), calls=%async_computation.1 | async-start | bytes 196608 | tf_op jit(solution)/shard_map/reduce_scatter | solution.py:162
  26.2 109.1 %collective-permute-start = (bf16[8,31,64]{2,0,1:T(8,128)(2,1)}, bf16[8,31,64]{2,0,1:T(8,128)(2,1)}, u32[]{:S(2)}, u32[]{:S(2)}) collective-permute-start(bf16[8,31,64]{2,0,1:T(8,128)(2,1)} %get-tuple-element.17), channel_id=1, source_target_pairs={{0,6},{2,8},{4,10},{6,12},{8,14},{10,16},{12,18},{14,20},{16,22},{... | collective-permute-start | bytes 95240 | tf_op jit(solution)/shard_map/ppermute | solution.py:14
  30.5 106.7 %collective-permute-start.1 = (bf16[8,31,64]{2,0,1:T(8,128)(2,1)}, bf16[8,31,64]{2,0,1:T(8,128)(2,1)}, u32[]{:S(2)}, u32[]{:S(2)}) collective-permute-start(bf16[8,31,64]{2,0,1:T(8,128)(2,1)} %get-tuple-element.17), channel_id=1, source_target_pairs={{0,4},{2,6},{4,8},{6,10},{8,12},{10,14},{12,16},{14,18},{16,20},{1... | collective-permute-start | bytes 95240 | tf_op jit(solution)/shard_map/ppermute | solution.py:14
  33.8 107.7 %collective-permute-start.2 = (bf16[8,31,64]{2,0,1:T(8,128)(2,1)}, bf16[8,31,64]{2,0,1:T(8,128)(2,1)S(1)}, u32[]{:S(2)}, u32[]{:S(2)}) collective-permute-start(bf16[8,31,64]{2,0,1:T(8,128)(2,1)} %get-tuple-element.17), channel_id=1, source_target_pairs={{0,2},{2,4},{4,6},{6,8},{8,10},{10,12},{12,14},{14,16},{16,18},{18... | collective-permute-start | bytes 95240 | tf_op jit(solution)/shard_map/ppermute | solution.py:14
  34.6 9.1 %collective-permute-start.6 = (bf16[8,1,64]{2,0,1:T(8,128)(2,1)}, bf16[8,1,64]{2,0,1:T(8,128)(2,1)}, u32[]{:S(2)}, u32[]{:S(2)}) collective-permute-start(bf16[8,1,64]{2,0,1:T(8,128)(2,1)} %bitcast.8), channel_id=1, source_target_pairs={{0,2},{2,0},{4,6},{6,4},{8,10},{10,8},{12,14},{14,12},{16,18},{18,... | collective-permute-start | bytes 3080 | tf_op jit(solution)/shard_map/ppermute | solution.py:20
  44.6 7.5 %collective-permute-start.7 = (bf16[8,1,64]{2,0,1:T(8,128)(2,1)S(1)}, bf16[8,1,64]{2,0,1:T(8,128)(2,1)S(1)}, u32[]{:S(2)}, u32[]{:S(2)}) collective-permute-start(bf16[8,1,64]{2,0,1:T(8,128)(2,1)S(1)} %bitcast.129), channel_id=1, source_target_pairs={{0,12},{2,14},{4,16},{6,18},{8,20},{10,22},{12,24},{14,26},{16,28}... | collective-permute-start | bytes 3080 | tf_op jit(solution)/shard_map/ppermute | solution.py:14
  52.1 27.5 %collective-permute-start.13 = (bf16[8,1,64]{2,0,1:T(8,128)(2,1)S(1)}, bf16[8,1,64]{2,0,1:T(8,128)(2,1)S(1)}, u32[]{:S(2)}, u32[]{:S(2)}) collective-permute-start(bf16[8,1,64]{2,0,1:T(8,128)(2,1)S(1)} %bitcast.130), channel_id=1, source_target_pairs={{0,4},{2,6},{4,0},{6,2},{8,12},{10,14},{12,8},{14,10},{16,20},{18,... | collective-permute-start | bytes 3080 | tf_op jit(solution)/shard_map/ppermute | solution.py:20
  52.1 9.4 %collective-permute-start.8 = (bf16[8,1,64]{2,0,1:T(8,128)(2,1)S(1)}, bf16[8,1,64]{2,0,1:T(8,128)(2,1)S(1)}, u32[]{:S(2)}, u32[]{:S(2)}) collective-permute-start(bf16[8,1,64]{2,0,1:T(8,128)(2,1)S(1)} %bitcast.131), channel_id=1, source_target_pairs={{0,8},{2,10},{4,12},{6,14},{8,16},{10,18},{12,20},{14,22},{16,24},... | collective-permute-start | bytes 3080 | tf_op jit(solution)/shard_map/ppermute | solution.py:14
  61.4 7.6 %collective-permute-start.9 = (bf16[8,1,64]{2,0,1:T(8,128)(2,1)S(1)}, bf16[8,1,64]{2,0,1:T(8,128)(2,1)S(1)}, u32[]{:S(2)}, u32[]{:S(2)}) collective-permute-start(bf16[8,1,64]{2,0,1:T(8,128)(2,1)S(1)} %bitcast.132), channel_id=1, source_target_pairs={{0,4},{2,6},{4,8},{6,10},{8,12},{10,14},{12,16},{14,18},{16,20},{1... | collective-permute-start | bytes 3080 | tf_op jit(solution)/shard_map/ppermute | solution.py:14
  69.0 3.6 %collective-permute-start.10 = (bf16[8,1,64]{2,0,1:T(8,128)(2,1)S(1)}, bf16[8,1,64]{2,0,1:T(8,128)(2,1)S(1)}, u32[]{:S(2)}, u32[]{:S(2)}) collective-permute-start(bf16[8,1,64]{2,0,1:T(8,128)(2,1)S(1)} %bitcast.133), channel_id=1, source_target_pairs={{0,252},{2,254},{4,0},{6,2},{8,4},{10,6},{12,8},{14,10},{16,12},{1... | collective-permute-start | bytes 3080 | tf_op jit(solution)/shard_map/ppermute | solution.py:14
  72.6 6.3 %collective-permute-start.11 = (bf16[8,1,64]{2,0,1:T(8,128)(2,1)S(1)}, bf16[8,1,64]{2,0,1:T(8,128)(2,1)S(1)}, u32[]{:S(2)}, u32[]{:S(2)}) collective-permute-start(bf16[8,1,64]{2,0,1:T(8,128)(2,1)S(1)} %bitcast.134), channel_id=1, source_target_pairs={{0,248},{2,250},{4,252},{6,254},{8,0},{10,2},{12,4},{14,6},{16,8},... | collective-permute-start | bytes 3080 | tf_op jit(solution)/shard_map/ppermute | solution.py:14
  79.0 7.5 %collective-permute-start.12 = (bf16[8,1,64]{2,0,1:T(8,128)(2,1)S(1)}, bf16[8,1,64]{2,0,1:T(8,128)(2,1)S(1)}, u32[]{:S(2)}, u32[]{:S(2)}) collective-permute-start(bf16[8,1,64]{2,0,1:T(8,128)(2,1)S(1)} %bitcast.135), channel_id=1, source_target_pairs={{0,244},{2,246},{4,248},{6,250},{8,252},{10,254},{12,0},{14,2},{16... | collective-permute-start | bytes 3080 | tf_op jit(solution)/shard_map/ppermute | solution.py:14
  79.6 69.0 %collective-permute-start.3 = (bf16[8,31,64]{2,0,1:T(8,128)(2,1)}, bf16[8,31,64]{2,0,1:T(8,128)(2,1)S(1)}, u32[]{:S(2)}, u32[]{:S(2)}) collective-permute-start(bf16[8,31,64]{2,0,1:T(8,128)(2,1)} %get-tuple-element.17), channel_id=1, source_target_pairs={{0,254},{2,0},{4,2},{6,4},{8,6},{10,8},{12,10},{14,12},{16,14},{18... | collective-permute-start | bytes 95240 | tf_op jit(solution)/shard_map/ppermute | solution.py:14
  86.5 9.7 %collective-permute-start.14 = (bf16[8,1,64]{2,0,1:T(8,128)(2,1)S(1)}, bf16[8,1,64]{2,0,1:T(8,128)(2,1)S(1)}, u32[]{:S(2)}, u32[]{:S(2)}) collective-permute-start(bf16[8,1,64]{2,0,1:T(8,128)(2,1)S(1)} %fusion.7), channel_id=1, source_target_pairs={{0,24},{2,26},{4,28},{6,30},{8,32},{10,34},{12,36},{14,38},{16,40}... | collective-permute-start | bytes 3080 | tf_op jit(solution)/shard_map/ppermute | solution.py:14
  96.1 4.8 %collective-permute-start.15 = (bf16[8,1,64]{2,0,1:T(8,128)(2,1)S(1)}, bf16[8,1,64]{2,0,1:T(8,128)(2,1)S(1)}, u32[]{:S(2)}, u32[]{:S(2)}) collective-permute-start(bf16[8,1,64]{2,0,1:T(8,128)(2,1)S(1)} %fusion.7), channel_id=1, source_target_pairs={{0,16},{2,18},{4,20},{6,22},{8,24},{10,26},{12,28},{14,30},{16,32}... | collective-permute-start | bytes 3080 | tf_op jit(solution)/shard_map/ppermute | solution.py:14
  100.9 9.4 %collective-permute-start.16 = (bf16[8,1,64]{2,0,1:T(8,128)(2,1)S(1)}, bf16[8,1,64]{2,0,1:T(8,128)(2,1)S(1)}, u32[]{:S(2)}, u32[]{:S(2)}) collective-permute-start(bf16[8,1,64]{2,0,1:T(8,128)(2,1)S(1)} %fusion.7), channel_id=1, source_target_pairs={{0,8},{2,10},{4,12},{6,14},{8,16},{10,18},{12,20},{14,22},{16,24},... | collective-permute-start | bytes 3080 | tf_op jit(solution)/shard_map/ppermute | solution.py:14
  110.3 6.3 %collective-permute-start.17 = (bf16[8,1,64]{2,0,1:T(8,128)(2,1)S(1)}, bf16[8,1,64]{2,0,1:T(8,128)(2,1)S(1)}, u32[]{:S(2)}, u32[]{:S(2)}) collective-permute-start(bf16[8,1,64]{2,0,1:T(8,128)(2,1)S(1)} %fusion.7), channel_id=1, source_target_pairs={{0,248},{2,250},{4,252},{6,254},{8,0},{10,2},{12,4},{14,6},{16,8},... | collective-permute-start | bytes 3080 | tf_op jit(solution)/shard_map/ppermute | solution.py:14
  116.6 2.7 %collective-permute-start.18 = (bf16[8,1,64]{2,0,1:T(8,128)(2,1)S(1)}, bf16[8,1,64]{2,0,1:T(8,128)(2,1)S(1)}, u32[]{:S(2)}, u32[]{:S(2)}) collective-permute-start(bf16[8,1,64]{2,0,1:T(8,128)(2,1)S(1)} %fusion.7), channel_id=1, source_target_pairs={{0,240},{2,242},{4,244},{6,246},{8,248},{10,250},{12,252},{14,254}... | collective-permute-start | bytes 3080 | tf_op jit(solution)/shard_map/ppermute | solution.py:14
  119.4 7.2 %collective-permute-start.19 = (bf16[8,1,64]{2,0,1:T(8,128)(2,1)S(1)}, bf16[8,1,64]{2,0,1:T(8,128)(2,1)S(1)}, u32[]{:S(2)}, u32[]{:S(2)}) collective-permute-start(bf16[8,1,64]{2,0,1:T(8,128)(2,1)S(1)} %fusion.7), channel_id=1, source_target_pairs={{0,232},{2,234},{4,236},{6,238},{8,240},{10,242},{12,244},{14,246}... | collective-permute-start | bytes 3080 | tf_op jit(solution)/shard_map/ppermute | solution.py:14
  126.6 22.6 %collective-permute-start.4 = (bf16[8,31,64]{2,0,1:T(8,128)(2,1)}, bf16[8,31,64]{2,0,1:T(8,128)(2,1)S(1)}, u32[]{:S(2)}, u32[]{:S(2)}) collective-permute-start(bf16[8,31,64]{2,0,1:T(8,128)(2,1)} %get-tuple-element.17), channel_id=1, source_target_pairs={{0,252},{2,254},{4,0},{6,2},{8,4},{10,6},{12,8},{14,10},{16,12},{1... | collective-permute-start | bytes 95240 | tf_op jit(solution)/shard_map/ppermute | solution.py:14
  135.3 14.6 %collective-permute-start.5 = (bf16[8,31,64]{2,0,1:T(8,128)(2,1)}, bf16[8,31,64]{2,0,1:T(8,128)(2,1)S(1)}, u32[]{:S(2)}, u32[]{:S(2)}) collective-permute-start(bf16[8,31,64]{2,0,1:T(8,128)(2,1)} %get-tuple-element.17), channel_id=1, source_target_pairs={{0,250},{2,252},{4,254},{6,0},{8,2},{10,4},{12,6},{14,8},{16,10},{... | collective-permute-start | bytes 95240 | tf_op jit(solution)/shard_map/ppermute | solution.py:14
  137.2 22.6 %collective-permute-start.20 = (bf16[8,2048]{0,1:T(8,128)(2,1)}, bf16[8,2048]{0,1:T(8,128)(2,1)}, u32[]{:S(2)}, u32[]{:S(2)}) collective-permute-start(bf16[8,2048]{0,1:T(8,128)(2,1)} %fusion.10), channel_id=1, source_target_pairs={{0,2},{2,4},{4,6},{6,8},{8,10},{10,12},{12,14},{14,16},{16,18},{18... | collective-permute-start | bytes 98312 | tf_op jit(solution)/shard_map/ppermute | solution.py:14
  141.5 19.5 %collective-permute-start.21 = (bf16[8,2048]{0,1:T(8,128)(2,1)}, bf16[8,2048]{0,1:T(8,128)(2,1)}, u32[]{:S(2)}, u32[]{:S(2)}) collective-permute-start(bf16[8,2048]{0,1:T(8,128)(2,1)} %fusion.10), channel_id=1, source_target_pairs={{0,254},{2,0},{4,2},{6,4},{8,6},{10,8},{12,10},{14,12},{16,14},{18... | collective-permute-start | bytes 98312 | tf_op jit(solution)/shard_map/ppermute | solution.py:14
  153.1 5.5 %copy-start.4 = (f32[8,128]{1,0:T(8,128)S(1)}, f32[8,128]{1,0:T(8,128)}, u32[]{:S(2)}) copy-start(f32[8,128]{1,0:T(8,128)} %fusion.9) | copy-start | bytes 12292
  181.2 22.8 %copy-start.1 = (bf16[16,64,128]{2,1,0:T(8,128)(2,1)S(1)}, bf16[16,64,128]{2,1,0:T(8,128)(2,1)}, u32[]{:S(2)}) copy-start(bf16[16,64,128]{2,1,0:T(8,128)(2,1)} %param.19) | copy-start | bytes 786436
Sparse Core Ops, SparseCore 0:
  187.5 16.4 reduce-scatter.1
where the time goes:
time: 216 us; the launch traced here: 213 us
  waiting for transfers between devices  69.2 us (32%)
  local copies, waits for them, and re-layouts  41.3 us (19%)
  starting transfers between devices  39.5 us (18%)
  matrix products  22.5 us (10%)
  blocking collectives  16.5 us (8%)
  between operations  13.6 us (6%)
  other arithmetic  9.94 us (5%)
    ppermute x20, waiting for transfers between devices, from_behind(): lax.ppermute(shard, axis, [(i, (i + by) % devices) for i in range(devices)])  57.4 us
    ppermute x20, starting transfers between devices, from_behind(): lax.ppermute(shard, axis, [(i, (i + by) % devices) for i in range(devices)])  38.7 us
    all_gather x1, blocking collectives, body(): whole = lax.all_gather(nearby, 'rhs', axis=0, tiled=True)  16.5 us
    reduce_scatter x1, waiting for transfers between devices, body(): lax.psum_scatter(terms.reshape(whole.shape[0], own_points), 'rhs', scatte...  11.8 us
    unnamed x35, local copies, waits for them, and re-layouts  10.4 us
    gather x2, local copies, waits for them, and re-layouts, body(): jnp.take(right_sides, point_order - my_place * own_points, axis=1)  9.96 us
    dot_general x8, matrix products, lift_terms(): jnp.einsum('nab,rnb->rna', matrices, vectors, preferred_element_type=jnp....  9.73 us
    dot_general x6, matrix products, lower_terms(): jnp.einsum('nab,rna->rnb', matrices, vectors, preferred_element_type=jnp....  7.3 us
  transfers between devices with their start and end apart: 23, of which 11 were waited for; matrix products, arithmetic and copies ran while one was open for 20% of the time, Pallas kernels for 0%

commit v1 on v0

v1 whole, which is shorter than its diff:
```python
import jax
import jax.numpy as jnp
from jax import lax
from jax.experimental import pallas as pl
from jax.experimental.pallas import tpu as pltpu
from jax.sharding import PartitionSpec as P

MESH = pl.DeviceIdType.MESH
F32 = jnp.float32
BF16 = jnp.bfloat16

DEVICES = 128
LEAVES = 16
RANK = 64
LANES = 128
COLS = 8
SLOTS = 14
FAR = 8
PAIRS = 15
ROWS = 2 * LEAVES
ZERO = 3 * ROWS
NEAR_ZERO = 3 * LEAVES
HALF = DEVICES // 2
QUARTER = DEVICES // 4


def dot_nt(left, right):
    return lax.dot_general(left, right, (((1,), (1,)), ((), ())), preferred_element_type=F32)


def dot_nn(left, right):
    return lax.dot_general(left, right, (((1,), (0,)), ((), ())), preferred_element_type=F32)


def wrap(value, size):
    return lax.rem(value + size, size)


def kernel(
    rs_h,
    order_h,
    basis_h,
    transfer_h,
    coupling_h,
    flist_h,
    fcount_h,
    ctr_h,
    ccp_h,
    clist_h,
    ccount_h,
    near_h,
    nlist_h,
    ncount_h,
    out_v,
    rs_v,
    order_v,
    basis_v,
    transfer_v,
    coupling_v,
    near_v,
    flist_v,
    fcount_v,
    nlist_v,
    ncount_v,
    ctr_v,
    ccp_v,
    clist_s,
    ccount_s,
    fid_v,
    nid_v,
    fid_s,
    nid_s,
    xs_v,
    us_v,
    xr_v,
    ur_v,
    cs_v,
    cr_v,
    xw_v,
    table_v,
    up_v,
    gu_v,
    fu_v,
    ysend_v,
    yrecv_v,
    in_sem,
    near_sem,
    id_sem,
    xsend_sem,
    xrecv_sem,
    usend_sem,
    urecv_sem,
    csend_sem,
    crecv_sem,
    ysend_sem,
    yrecv_sem,
):
    me = lax.axis_index("leaf")
    core = lax.axis_index("rhs")
    other = 1 - core
    quad = lax.div(me, 4)
    in_quad = lax.rem(me, 4)
    duo = lax.div(me, 2)
    in_duo = lax.rem(me, 2)
    turn = 1 - 2 * in_duo
    duo_turn = 1 - 2 * lax.rem(duo, 2)
    quad_turn = 1 - 2 * lax.rem(quad, 2)
    quad_from = [wrap(quad + d, QUARTER) for d in (-2, 2, 3 * quad_turn)]
    duo_from = [wrap(duo + d, HALF) for d in (-2, 2, 3 * duo_turn)]
    quad_to = [quad_from[1], quad_from[0], quad_from[2]]
    duo_to = [duo_from[1], duo_from[0], duo_from[2]]
    one_to = [wrap(me + d, DEVICES) for d in (2, -2, 3 * turn)]
    root_sends = []
    for n in range(3):
        for i in range(4):
            root_sends.append((4 * quad_to[n] + i, 4 * n + in_quad))
    for n in range(3):
        for i in range(2):
            root_sends.append((2 * duo_to[n] + i, 12 + 2 * n + in_duo))
    for n in range(3):
        root_sends.append((one_to[n], 18 + n))
    left = wrap(me - 1, DEVICES)
    right = wrap(me + 1, DEVICES)
    point_sends = [(right, core, 0), (left, core, 1), (right, other, 2), (left, other, 3), (me, other, 4)]

    def fetch(source, target, sem):
        copy = pltpu.make_async_copy(source, target, sem)
        copy.start()
        return copy

    get_order = fetch(order_h, order_v, in_sem.at[0])
    get_rs = fetch(rs_h, rs_v, in_sem.at[1])
    get_basis = fetch(basis_h, basis_v, in_sem.at[2])
    get_transfer = fetch(transfer_h, transfer_v, in_sem.at[3])
    get_lists = [
        fetch(nlist_h, nlist_v, in_sem.at[4]),
        fetch(ncount_h, ncount_v, in_sem.at[5]),
        fetch(flist_h, flist_v, in_sem.at[6]),
        fetch(fcount_h, fcount_v, in_sem.at[7]),
    ]
    get_coarse = [fetch(clist_h, clist_s, in_sem.at[8]), fetch(ccount_h, ccount_s, in_sem.at[9])]
    for device_at, device_core in [(to, core) for to, _ in root_sends] + [(to, at) for to, at, _ in point_sends]:
        pl.semaphore_signal(
            pltpu.get_barrier_semaphore(),
            inc=1,
            device_id=(device_at, device_core),
            device_id_type=MESH,
        )
    for j in range(4):
        fetch(near_h.at[j], near_v.at[j], near_sem.at[j])
    for n in range(3):
        fetch(ctr_h.at[pl.ds(2 * quad_from[n], 2)], ctr_v.at[pl.ds(2 * n, 2)], in_sem.at[10])
        fetch(ctr_h.at[pl.ds(duo_from[n], 1)], ctr_v.at[pl.ds(6 + n, 1)], in_sem.at[10])
        fetch(ctr_h.at[pl.ds(HALF + quad_from[n], 1)], ctr_v.at[pl.ds(9 + n, 1)], in_sem.at[10])
    fetch(ctr_h.at[pl.ds(duo, 1)], ctr_v.at[pl.ds(12, 1)], in_sem.at[10])
    fetch(ctr_h.at[pl.ds(HALF + quad, 1)], ctr_v.at[pl.ds(13, 1)], in_sem.at[10])
    fetch(ccp_h.at[pl.ds(duo, 1)], ccp_v.at[pl.ds(0, 1)], in_sem.at[11])
    fetch(ccp_h.at[pl.ds(HALF + quad, 1)], ccp_v.at[pl.ds(1, 1)], in_sem.at[11])
    for j in range(4, LEAVES):
        fetch(near_h.at[j], near_v.at[j], near_sem.at[j])
    get_coupling = fetch(coupling_h, coupling_v, in_sem.at[12])

    low = lax.broadcasted_iota(jnp.int32, (COLS, LANES), 1) < RANK
    low16 = lax.broadcasted_iota(jnp.int32, (2 * COLS, LANES), 1) < RANK
    top16 = lax.broadcasted_iota(jnp.int32, (2 * COLS, LANES), 0) < COLS
    diagonal = low16 == top16

    def both(first, second):
        return jnp.concatenate([first, second], axis=0)

    def meet(first, second):
        return jnp.where(low, first, second)

    def flip(pair):
        return pltpu.roll(pair, RANK, 1)

    def join(product):
        return jnp.where(low, product[:COLS], product[COLS:])

    get_order.wait()
    get_rs.wait()
    place = order_v[...] - me * (LEAVES * LANES)
    for j in range(0, LEAVES, 2):
        blocks = []
        for i in (j, j + 1):
            here = jnp.broadcast_to(place[i : i + 1], (COLS, LANES))
            chunk = here // LANES
            lane = here % LANES
            block = jnp.take_along_axis(rs_v[:, 0:LANES], lane, axis=1, mode="promise_in_bounds")
            for c in range(1, LEAVES):
                found = jnp.take_along_axis(
                    rs_v[:, c * LANES : (c + 1) * LANES], lane, axis=1, mode="promise_in_bounds"
                )
                block = jnp.where(chunk == c, found, block)
            blocks.append(block)
        xs_v[j // 2] = both(*blocks).astype(BF16)

    pl.semaphore_wait(pltpu.get_barrier_semaphore(), len(root_sends) + len(point_sends))

    def remote(source, target, send_sem, recv_sem, device_at, device_core):
        return pltpu.make_async_remote_copy(
            src_ref=source,
            dst_ref=target,
            send_sem=send_sem,
            recv_sem=recv_sem,
            device_id=(device_at, device_core),
            device_id_type=MESH,
        )

    sent = []
    for device_at, device_core, slot in point_sends:
        copy = remote(
            xs_v, xr_v.at[slot], xsend_sem.at[slot], xrecv_sem.at[slot], device_at, device_core
        )
        copy.start()
        sent.append(copy)

    get_basis.wait()
    get_transfer.wait()
    own = ROWS
    for p in range(LEAVES // 2):
        matrices = basis_v[2 * p : 2 * p + 2].reshape(LANES, LANES)
        pair = join(dot_nt(xs_v[p], matrices))
        up_v[p] = pair
        table_v[own + 2 * p] = pair
        table_v[own + 2 * p + 1] = flip(pair)
    first = 0
    for width in (8, 4, 2):
        for p in range(width // 2):
            tile = both(up_v[first + 2 * p], up_v[first + 2 * p + 1]).astype(BF16)
            us_v[first // 2 + p] = tile
            row = first + 2 * p
            matrices = transfer_v[row : row + 2].reshape(LANES, LANES)
            pair = join(dot_nt(tile, matrices))
            at = first + width + p
            up_v[at] = pair
            table_v[own + 2 * at] = pair
            table_v[own + 2 * at + 1] = flip(pair)
        first += width
    last = both(up_v[14], jnp.zeros((COLS, LANES), F32)).astype(BF16)
    us_v[7] = last
    sides = []
    for slot, device_at in ((0, right), (1, left)):
        copy = remote(us_v, ur_v.at[slot], usend_sem.at[slot], urecv_sem.at[slot], device_at, core)
        copy.start()
        sides.append(copy)
    root = transfer_v[14]
    cs_v[...] = dot_nt(last, both(root, root))[:COLS].astype(BF16).astype(F32)
    for device_at, slot in root_sends:
        remote(cs_v, cr_v.at[slot], csend_sem, crecv_sem, device_at, core).start()

    for copy in get_lists:
        copy.wait()
    square = lax.broadcasted_iota(jnp.int32, (LEAVES, LEAVES), 0) == lax.broadcasted_iota(
        jnp.int32, (LEAVES, LEAVES), 1
    )
    counts = jnp.broadcast_to(ncount_v[...], (LEAVES, LEAVES))
    counts = jnp.sum(jnp.where(square, counts, 0), axis=1, keepdims=True)
    slot_at = lax.broadcasted_iota(jnp.int32, (LEAVES, SLOTS), 1) + core * SLOTS
    nid_v[...] = jnp.where(slot_at < counts, nlist_v[...] - (me - 1) * LEAVES, NEAR_ZERO)
    node = lax.broadcasted_iota(jnp.int32, (FAR, ROWS - 1), 1)
    slot_at = lax.broadcasted_iota(jnp.int32, (FAR, ROWS - 1), 0)
    entry = flist_v[...]
    row = jnp.zeros_like(entry)
    for height in range(4):
        width = LEAVES >> height
        start = ROWS - 2 * width
        side = entry // width - me + 1
        inside = (node >= start) & (node < start + width)
        row = jnp.where(inside, side * ROWS + start + entry % width, row)
    row = row + jnp.where(slot_at % 2 == 0, 0, 1 - 2 * (row % 2))
    step = entry - me
    root_row = jnp.where(step == -2, 0, jnp.where(step == 2, 1, 2))
    row = jnp.where(node == ROWS - 2, root_row, row)
    live = slot_at < fcount_v[...]
    fid_v[...] = jnp.where(live, row, jnp.where(node == ROWS - 2, 3, ZERO))
    put_near = fetch(nid_v, nid_s, id_sem.at[0])
    put_far = fetch(fid_v, fid_s, id_sem.at[1])
    zero = jnp.zeros((COLS, LANES), F32)
    table_v[ZERO] = zero
    xw_v[NEAR_ZERO] = jnp.zeros((2 * COLS, LANES), BF16)
    put_near.wait()
    put_far.wait()

    for copy in sent:
        copy.wait()

    def arrange(base, mine, theirs):
        for p in range(LEAVES // 2):
            a = mine[p].astype(F32)
            b = theirs[p].astype(F32)
            xw_v[base + 2 * p] = both(a[:COLS], b[:COLS]).astype(BF16)
            xw_v[base + 2 * p + 1] = both(a[COLS:], b[COLS:]).astype(BF16)

    arrange(0, xr_v.at[0], xr_v.at[2])
    arrange(LEAVES, xs_v, xr_v.at[4])
    arrange(2 * LEAVES, xr_v.at[1], xr_v.at[3])

    def near_leaf(j, carry):
        pltpu.make_async_copy(near_h.at[j], near_v.at[j], near_sem.at[j]).wait()
        total = jnp.zeros((2 * COLS, LANES), F32)
        for s in range(SLOTS):
            total += dot_nt(xw_v[nid_s[j, s]], near_v[j, s])
        yown = total[:COLS]
        out_v[:, pl.ds(pl.multiple_of(j * LANES, LANES), LANES)] = yown
        ysend_v[j] = total[COLS:]
        return carry

    lax.fori_loop(0, LEAVES, near_leaf, 0)
    send_near = remote(ysend_v, yrecv_v, ysend_sem, yrecv_sem, me, other)
    send_near.start()

    for copy in sides:
        copy.wait()
    for slot, base in ((0, 0), (1, 2 * ROWS)):
        for t in range(8):
            tile = ur_v[slot, t].astype(F32)
            for half in range(2):
                pair = tile[half * COLS : (half + 1) * COLS]
                table_v[base + 4 * t + 2 * half] = pair
                table_v[base + 4 * t + 2 * half + 1] = flip(pair)

    get_coupling.wait()

    def couple(p, carry):
        total = jnp.zeros((2 * COLS, LANES), F32)
        matrices = coupling_v[pl.ds(2 * p, 2)].reshape(LANES, FAR * RANK)
        for t in range(FAR // 2):
            picked = both(
                meet(table_v[fid_s[2 * t, 2 * p]], table_v[fid_s[2 * t + 1, 2 * p]]),
                meet(table_v[fid_s[2 * t, 2 * p + 1]], table_v[fid_s[2 * t + 1, 2 * p + 1]]),
            ).astype(BF16)
            total += dot_nt(picked, matrices[:, t * LANES : (t + 1) * LANES])
        gu_v[p] = join(total)
        return carry

    lax.fori_loop(0, PAIRS, couple, 0)

    pltpu.make_async_copy(ctr_h.at[pl.ds(0, 14)], ctr_v, in_sem.at[10]).wait()
    pltpu.make_async_copy(ccp_h.at[pl.ds(0, 2)], ccp_v, in_sem.at[11]).wait()
    for copy in get_coarse:
        copy.wait()
    everyone = remote(cr_v, cr_v, csend_sem, crecv_sem, me, other)
    everyone.wait_send()
    everyone.wait_recv()
    for k in range(3):
        up_v[4 * k + 3] = zero
    for n in range(3):
        pair = both(meet(cr_v[4 * n], cr_v[4 * n + 1]), meet(cr_v[4 * n + 2], cr_v[4 * n + 3]))
        upper = join(dot_nt(pair.astype(BF16), ctr_v[2 * n : 2 * n + 2].reshape(LANES, LANES)))
        matrix = ctr_v[9 + n]
        up_v[n] = dot_nt(both(upper, upper).astype(BF16), both(matrix, matrix))[:COLS]
        pair = meet(cr_v[12 + 2 * n], cr_v[13 + 2 * n])
        matrix = ctr_v[6 + n]
        up_v[4 + n] = dot_nt(both(pair, pair).astype(BF16), both(matrix, matrix))[:COLS]
        up_v[8 + n] = cr_v[18 + n]

    def upper_terms(matrix, at, node_here, base):
        rows = []
        for s in range(3):
            step = clist_s[s, at] - node_here
            row = jnp.where(step == -2, 0, jnp.where(step == 2, 1, 2))
            rows.append(base + jnp.where(s < ccount_s[at], row, 3))
        pair = meet(up_v[rows[0]], up_v[rows[1]])
        third = up_v[rows[2]]
        total = dot_nt(both(pair, pair).astype(BF16), matrix[:, :LANES])
        total += dot_nt(both(third, third)[:, :RANK].astype(BF16), matrix[:, LANES:])
        return total

    g6 = upper_terms(ccp_v[1], HALF + quad, quad, 0)
    g5 = upper_terms(ccp_v[0], duo, duo, 4)

    def pick_child(product, side):
        return jnp.where(side == 0, product, pltpu.roll(product, RANK, 1))[:, :RANK]

    field = g6.astype(BF16)
    field = g5 + pick_child(dot_nn(field, ctr_v[13]), lax.rem(duo, 2))
    field = field.astype(BF16)
    matrix = coupling_v[ROWS - 2]
    pair = meet(up_v[8 + fid_s[0, ROWS - 2]], up_v[8 + fid_s[1, ROWS - 2]])
    third = up_v[8 + fid_s[2, ROWS - 2]]
    g4 = dot_nt(both(pair, pair).astype(BF16), matrix[:, :LANES])
    g4 += dot_nt(both(third, third)[:, :RANK].astype(BF16), matrix[:, LANES : LANES + RANK])
    field = g4 + pick_child(dot_nn(field, ctr_v[12]), in_duo)
    fu_v[14] = gu_v[14] + dot_nn(field.astype(BF16), transfer_v[14])[:COLS]
    for first, width in ((12, 2), (8, 4), (0, 8)):
        for p in range(width // 2):
            pair = fu_v[first + width + p]
            spread = jnp.where(diagonal, both(pair, pair), 0.0).astype(BF16)
            row = first + 2 * p
            down = dot_nn(spread, transfer_v[row : row + 2].reshape(LANES, LANES))
            fu_v[row] = gu_v[row] + down[:COLS]
            fu_v[row + 1] = gu_v[row + 1] + down[COLS:]
    send_near.wait()
    for p in range(LEAVES // 2):
        pair = fu_v[p]
        spread = jnp.where(diagonal, both(pair, pair), 0.0).astype(BF16)
        far = dot_nn(spread, basis_v[2 * p : 2 * p + 2].reshape(LANES, LANES))
        for half in range(2):
            j = 2 * p + half
            columns = slice(j * LANES, (j + 1) * LANES)
            out_v[:, columns] += far[half * COLS : (half + 1) * COLS] + yrecv_v[j]


def body(
    right_sides,
    point_order,
    leaf_basis,
    transfer,
    coupling,
    far_list,
    far_count,
    coarse_transfer,
    coarse_coupling,
    coarse_list,
    coarse_count,
    near_block,
    near_list,
    near_count,
):
    tile = (2 * COLS, LANES)
    dma = pltpu.SemaphoreType.DMA
    return pl.pallas_call(
        kernel,
        out_shape=jax.ShapeDtypeStruct((COLS, LEAVES * LANES), F32),
        in_specs=[pl.BlockSpec(memory_space=pltpu.HBM)] * 14,
        out_specs=pl.BlockSpec(memory_space=pltpu.VMEM),
        scratch_shapes=[
            pltpu.VMEM((COLS, LEAVES * LANES), F32),
            pltpu.VMEM((LEAVES, LANES), jnp.int32),
            pltpu.VMEM((LEAVES, RANK, LANES), BF16),
            pltpu.VMEM((LEAVES - 1, RANK, LANES), BF16),
            pltpu.VMEM((ROWS - 1, RANK, FAR * RANK), BF16),
            pltpu.VMEM((LEAVES, SLOTS, LANES, LANES), BF16),
            pltpu.VMEM((FAR, ROWS - 1), jnp.int32),
            pltpu.VMEM((1, ROWS - 1), jnp.int32),
            pltpu.VMEM((LEAVES, SLOTS), jnp.int32),
            pltpu.VMEM((1, LEAVES), jnp.int32),
            pltpu.VMEM((14, RANK, LANES), BF16),
            pltpu.VMEM((2, RANK, 3 * RANK), BF16),
            pltpu.SMEM((3, 96), jnp.int32),
            pltpu.SMEM((96,), jnp.int32),
            pltpu.VMEM((FAR, ROWS - 1), jnp.int32),
            pltpu.VMEM((LEAVES, SLOTS), jnp.int32),
            pltpu.SMEM((FAR, ROWS - 1), jnp.int32),
            pltpu.SMEM((LEAVES, SLOTS), jnp.int32),
            pltpu.VMEM((LEAVES // 2,) + tile, BF16),
            pltpu.VMEM((LEAVES // 2,) + tile, BF16),
            pltpu.VMEM((5, LEAVES // 2) + tile, BF16),
            pltpu.VMEM((2, LEAVES // 2) + tile, BF16),
            pltpu.VMEM((COLS, LANES), F32),
            pltpu.VMEM((21, COLS, LANES), F32),
            pltpu.VMEM((3 * LEAVES + 1,) + tile, BF16),
            pltpu.VMEM((ZERO + 1, COLS, LANES), F32),
            pltpu.VMEM((PAIRS, COLS, LANES), F32),
            pltpu.VMEM((PAIRS, COLS, LANES), F32),
            pltpu.VMEM((PAIRS, COLS, LANES), F32),
            pltpu.VMEM((LEAVES, COLS, LANES), F32),
            pltpu.VMEM((LEAVES, COLS, LANES), F32),
            dma((13,)),
            dma((LEAVES,)),
            dma((2,)),
            dma((5,)),
            dma((5,)),
            dma((2,)),
            dma((2,)),
            dma,
            dma,
            dma,
            dma,
        ],
        compiler_params=pltpu.CompilerParams(
            collective_id=0, has_side_effects=True, vmem_limit_bytes=56 << 20
        ),
    )(
        right_sides,
        point_order.reshape(LEAVES, LANES),
        leaf_basis,
        transfer,
        coupling,
        far_list.T,
        far_count.reshape(1, ROWS - 1),
        coarse_transfer,
        coarse_coupling,
        coarse_list.T,
        coarse_count,
        near_block,
        near_list,
        near_count.reshape(1, LEAVES),
    )


def solution(mesh):
    return jax.shard_map(
        body,
        mesh=mesh,
        in_specs=(
            P("rhs", "leaf"),
            P("leaf"),
            P("leaf", None, None),
            P("leaf", None, None),
            P("leaf", None, None),
            P("leaf", None),
            P("leaf"),
            P(),
            P(),
            P(),
            P(),
            P("leaf", "rhs", None, None),
            P("leaf", "rhs"),
            P("leaf"),
        ),
        out_specs=P("rhs", "leaf"),
        check_vma=False,
    )
```

time: 216 us -> 30.1 us (0.14)
  the two profiles are of different devices: /device:TPU:7 before, /device:TPU:1 now
where the time goes in v1:
time: 30.1 us; the launch traced here: 29.9 us
  Pallas kernels  28.5 us (95%)
  local copies, waits for them, and re-layouts  1.47 us (5%)
    pallas_call x1, Pallas kernels, body(): pl.pallas_call(kernel, out_shape=jax.ShapeDtypeStruct((COLS, LEAVES * LAN...  28.5 us
    unnamed x1, local copies, waits for them, and re-layouts  1.47 us

profile of v1, /device:TPU:1, one launch (start us, length us, event | category | flops | bytes accessed | tf_op | source)
XLA Modules:
  0.0 29.9 jit_solution(6190056260930550942)
XLA Ops:
  0.0 28.5 %shard_map.136 = f32[8,2048]{1,0:T(8,128)} custom-call(f32[8,2048]{1,0:T(8,128)} %rs_h.1, s32[16,128]{1,0:T(8,128)} %bitcast.5, bf16[16,64,128]{2,1,0:T(8,128)(2,1)} %basis_h.1, bf16[15,64,128]{2,1,0:T(8,128)(2,1)} %transfer_h.1, bf16[31,64,512]{2,1,0:T(8,128)(2,1)} %coupling_h.1, s32[8,31]{1,0:T(8,128)} %bitcast.6, s32[1,31]{1,0:T(1,128)} %bitcast.8, ...), custom_call_target="tpu_custom_call" | custom-call | tf_op jit(solution)/shard_map/pallas_call | solution.py:423
  28.5 1.5 %copy.16 = f32[8,2048]{1,0:T(8,128)} copy(f32[8,2048]{1,0:T(8,128)} %shard_map.136) | data formatting | bytes 131072

commit v2 on v1

--- a/solution.py
+++ b/solution.py
@@ -20,6 +20,7 @@
 ROWS = 2 * LEAVES
 ZERO = 3 * ROWS
 NEAR_ZERO = 3 * LEAVES
+NEAR_STEP = 8
 HALF = DEVICES // 2
 QUARTER = DEVICES // 4
 
@@ -34,6 +35,17 @@
 
 def wrap(value, size):
     return lax.rem(value + size, size)
+
+
+def within(value, size):
+    return (value >= 0) & (value < size)
+
+
+def when(flag, do):
+    if flag is None:
+        do()
+    else:
+        pl.when(flag)(do)
 
 
 def kernel(
@@ -80,7 +92,10 @@
     table_v,
     up_v,
     gu_v,
-    fu_v,
+    reach_v,
+    rise_v,
+    fall_v,
+    yown_v,
     ysend_v,
     yrecv_v,
     in_sem,
@@ -107,21 +122,29 @@
     quad_turn = 1 - 2 * lax.rem(quad, 2)
     quad_from = [wrap(quad + d, QUARTER) for d in (-2, 2, 3 * quad_turn)]
     duo_from = [wrap(duo + d, HALF) for d in (-2, 2, 3 * duo_turn)]
-    quad_to = [quad_from[1], quad_from[0], quad_from[2]]
-    duo_to = [duo_from[1], duo_from[0], duo_from[2]]
-    one_to = [wrap(me + d, DEVICES) for d in (2, -2, 3 * turn)]
-    root_sends = []
-    for n in range(3):
-        for i in range(4):
-            root_sends.append((4 * quad_to[n] + i, 4 * n + in_quad))
-    for n in range(3):
-        for i in range(2):
-            root_sends.append((2 * duo_to[n] + i, 12 + 2 * n + in_duo))
-    for n in range(3):
-        root_sends.append((one_to[n], 18 + n))
-    left = wrap(me - 1, DEVICES)
-    right = wrap(me + 1, DEVICES)
-    point_sends = [(right, core, 0), (left, core, 1), (right, other, 2), (left, other, 3), (me, other, 4)]
+    groups = []
+    for n, (send_by, get_by) in enumerate(((2, -2), (-2, 2), (0, 0))):
+        for base, size, node, node_turn, nodes, place_in in (
+            (0, 4, quad, quad_turn, QUARTER, in_quad),
+            (12, 2, duo, duo_turn, HALF, in_duo),
+            (18, 1, me, turn, DEVICES, 0),
+        ):
+            to = node + (send_by if n < 2 else 3 * node_turn)
+            source = node + (get_by if n < 2 else 3 * node_turn)
+            groups.append(
+                (base + size * n, size, size * to, place_in, within(to, nodes), within(source, nodes))
+            )
+    left = me - 1
+    right = me + 1
+    has_left = left >= 0
+    has_right = right < DEVICES
+    point_sends = [
+        (right, core, 0, has_right, 1),
+        (left, core, 1, has_left, 0),
+        (right, other, 2, has_right, 3),
+        (left, other, 3, has_left, 2),
+        (me, other, 4, None, 4),
+    ]
 
     def fetch(source, target, sem):
         copy = pltpu.make_async_copy(source, target, sem)
@@ -139,13 +162,27 @@
         fetch(fcount_h, fcount_v, in_sem.at[7]),
     ]
     get_coarse = [fetch(clist_h, clist_s, in_sem.at[8]), fetch(ccount_h, ccount_s, in_sem.at[9])]
-    for device_at, device_core in [(to, core) for to, _ in root_sends] + [(to, at) for to, at, _ in point_sends]:
+    def greet(device_at, device_core):
         pl.semaphore_signal(
             pltpu.get_barrier_semaphore(),
             inc=1,
             device_id=(device_at, device_core),
             device_id_type=MESH,
         )
+
+    peers = 1
+    for device_at, device_core, _, there, _ in point_sends:
+        when(there, lambda: greet(device_at, device_core))
+        if there is not None:
+            peers = peers + jnp.where(there, 1, 0)
+    for _, size, to, _, there, source_there in groups:
+
+        def greet_all():
+            for i in range(size):
+                greet(to + i, core)
+
+        when(there, greet_all)
+        peers = peers + jnp.where(source_there, size, 0)
     for j in range(4):
         fetch(near_h.at[j], near_v.at[j], near_sem.at[j])
     for n in range(3):
@@ -194,26 +231,6 @@
                 block = jnp.where(chunk == c, found, block)
             blocks.append(block)
         xs_v[j // 2] = both(*blocks).astype(BF16)
-
-    pl.semaphore_wait(pltpu.get_barrier_semaphore(), len(root_sends) + len(point_sends))
-
-    def remote(source, target, send_sem, recv_sem, device_at, device_core):
-        return pltpu.make_async_remote_copy(
-            src_ref=source,
-            dst_ref=target,
-            send_sem=send_sem,
-            recv_sem=recv_sem,
-            device_id=(device_at, device_core),
-            device_id_type=MESH,
-        )
-
-    sent = []
-    for device_at, device_core, slot in point_sends:
-        copy = remote(
-            xs_v, xr_v.at[slot], xsend_sem.at[slot], xrecv_sem.at[slot], device_at, device_core
-        )
-        copy.start()
-        sent.append(copy)
 
     get_basis.wait()
     get_transfer.wait()
@@ -239,16 +256,8 @@
         first += width
     last = both(up_v[14], jnp.zeros((COLS, LANES), F32)).astype(BF16)
     us_v[7] = last
-    sides = []
-    for slot, device_at in ((0, right), (1, left)):
-        copy = remote(us_v, ur_v.at[slot], usend_sem.at[slot], urecv_sem.at[slot], device_at, core)
-        copy.start()
-        sides.append(copy)
     root = transfer_v[14]
     cs_v[...] = dot_nt(last, both(root, root))[:COLS].astype(BF16).astype(F32)
-    for device_at, slot in root_sends:
-        remote(cs_v, cr_v.at[slot], csend_sem, crecv_sem, device_at, core).start()
-
     for copy in get_lists:
         copy.wait()
     square = lax.broadcasted_iota(jnp.int32, (LEAVES, LEAVES), 0) == lax.broadcasted_iota(
@@ -279,39 +288,88 @@
     zero = jnp.zeros((COLS, LANES), F32)
     table_v[ZERO] = zero
     xw_v[NEAR_ZERO] = jnp.zeros((2 * COLS, LANES), BF16)
+
+    def remote(source, target, send_sem, recv_sem, device_at, device_core):
+        return pltpu.make_async_remote_copy(
+            src_ref=source,
+            dst_ref=target,
+            send_sem=send_sem,
+            recv_sem=recv_sem,
+            device_id=(device_at, device_core),
+            device_id_type=MESH,
+        )
+
+    def send_points(slot, device_at, device_core):
+        return remote(
+            xs_v, xr_v.at[slot], xsend_sem.at[slot], xrecv_sem.at[slot], device_at, device_core
+        )
+
+    def send_side(slot, device_at):
+        return remote(us_v, ur_v.at[slot], usend_sem.at[slot], urecv_sem.at[slot], device_at, core)
+
+    pl.semaphore_wait(pltpu.get_barrier_semaphore(), peers)
+    side_sends = ((0, right, has_right, 1), (1, left, has_left, 0))
+    for slot, device_at, there, _ in side_sends:
+        when(there, lambda: send_side(slot, device_at).start())
+    for device_at, device_core, slot, there, _ in point_sends:
+        when(there, lambda: send_points(slot, device_at, device_core).start())
+    for k, (first, size, to, place_in, there, _) in enumerate(groups):
+
+        def send_root():
+            for i in range(size):
+                target = cr_v.at[first + place_in]
+                remote(cs_v, target, csend_sem.at[k], crecv_sem.at[k], to + i, core).start()
+
+        when(there, send_root)
     put_near.wait()
     put_far.wait()
 
-    for copy in sent:
+    def spread(pair, mask):
+        return jnp.where(mask, both(pair, pair), 0.0).astype(BF16)
+
+    low128 = lax.broadcasted_iota(jnp.int32, (LANES, LANES), 1) < RANK
+    top128 = lax.broadcasted_iota(jnp.int32, (LANES, LANES), 0) < RANK
+    diagonal128 = low128 == top128
+    chains = {14: transfer_v[14].astype(F32)}
+    for first, width in ((12, 2), (8, 4), (0, 8)):
+        for p in range(width // 2):
+            row = first + 2 * p
+            matrices = transfer_v[row : row + 2].reshape(LANES, LANES)
+            product = dot_nn(spread(chains[first + width + p], diagonal128), matrices)
+            chains[row] = product[:RANK]
+            chains[row + 1] = product[RANK:]
+    for p in range(LEAVES // 2):
+        matrices = basis_v[2 * p : 2 * p + 2].reshape(LANES, LANES)
+        product = dot_nn(spread(chains[p], diagonal128), matrices).astype(BF16)
+        reach_v[:, 2 * p * LANES : (2 * p + 1) * LANES] = product[:RANK]
+        reach_v[:, (2 * p + 1) * LANES : (2 * p + 2) * LANES] = product[RANK:]
+    pltpu.make_async_copy(ctr_h.at[pl.ds(0, 14)], ctr_v, in_sem.at[10]).wait()
+    pltpu.make_async_copy(ccp_h.at[pl.ds(0, 2)], ccp_v, in_sem.at[11]).wait()
+    for copy in get_coarse:
         copy.wait()
-
-    def arrange(base, mine, theirs):
-        for p in range(LEAVES // 2):
-            a = mine[p].astype(F32)
-            b = theirs[p].astype(F32)
-            xw_v[base + 2 * p] = both(a[:COLS], b[:COLS]).astype(BF16)
-            xw_v[base + 2 * p + 1] = both(a[COLS:], b[COLS:]).astype(BF16)
-
-    arrange(0, xr_v.at[0], xr_v.at[2])
-    arrange(LEAVES, xs_v, xr_v.at[4])
-    arrange(2 * LEAVES, xr_v.at[1], xr_v.at[3])
-
-    def near_leaf(j, carry):
-        pltpu.make_async_copy(near_h.at[j], near_v.at[j], near_sem.at[j]).wait()
-        total = jnp.zeros((2 * COLS, LANES), F32)
-        for s in range(SLOTS):
-            total += dot_nt(xw_v[nid_s[j, s]], near_v[j, s])
-        yown = total[:COLS]
-        out_v[:, pl.ds(pl.multiple_of(j * LANES, LANES), LANES)] = yown
-        ysend_v[j] = total[COLS:]
-        return carry
-
-    lax.fori_loop(0, LEAVES, near_leaf, 0)
-    send_near = remote(ysend_v, yrecv_v, ysend_sem, yrecv_sem, me, other)
-    send_near.start()
-
-    for copy in sides:
-        copy.wait()
+    for n in range(3):
+        matrix = ctr_v[9 + n].astype(F32)
+        product = dot_nn(
+            spread(matrix, diagonal128), ctr_v[2 * n : 2 * n + 2].reshape(LANES, LANES)
+        ).astype(BF16)
+        rise_v[n, :, :LANES] = product[:RANK]
+        rise_v[n, :, LANES:] = product[RANK:]
+    duo_matrix = ctr_v[12].astype(F32)
+    duo_matrix = jnp.where(in_duo == 0, duo_matrix, flip(duo_matrix)).astype(BF16)
+    quad_matrix = ctr_v[13].astype(F32)
+    quad_matrix = jnp.where(lax.rem(duo, 2) == 0, quad_matrix, flip(quad_matrix)).astype(BF16)
+    fall_v[:RANK] = dot_nn(quad_matrix[:, :RANK], duo_matrix).astype(BF16)
+    fall_v[RANK:] = duo_matrix
+
+    def zero_side(slot):
+        def fill():
+            ur_v[slot] = jnp.zeros(ur_v.shape[1:], BF16)
+
+        return fill
+
+    for slot, device_at, there, source_slot in side_sends:
+        pl.when(jnp.logical_not(there))(zero_side(source_slot))
+        when(there, lambda: send_side(source_slot, device_at).wait_recv())
     for slot, base in ((0, 0), (1, 2 * ROWS)):
         for t in range(8):
             tile = ur_v[slot, t].astype(F32)
@@ -322,84 +380,131 @@
 
     get_coupling.wait()
 
-    def couple(p, carry):
-        total = jnp.zeros((2 * COLS, LANES), F32)
-        matrices = coupling_v[pl.ds(2 * p, 2)].reshape(LANES, FAR * RANK)
-        for t in range(FAR // 2):
-            picked = both(
-                meet(table_v[fid_s[2 * t, 2 * p]], table_v[fid_s[2 * t + 1, 2 * p]]),
-                meet(table_v[fid_s[2 * t, 2 * p + 1]], table_v[fid_s[2 * t + 1, 2 * p + 1]]),
-            ).astype(BF16)
-            total += dot_nt(picked, matrices[:, t * LANES : (t + 1) * LANES])
-        gu_v[p] = join(total)
+    for p in range(PAIRS):
+        matrices = coupling_v[2 * p : 2 * p + 2].reshape(LANES, FAR * RANK)
+        picked = []
+        for node in (2 * p, 2 * p + 1):
+            picked.append(
+                jnp.concatenate(
+                    [
+                        meet(table_v[fid_s[2 * t, node]], table_v[fid_s[2 * t + 1, node]])
+                        for t in range(FAR // 2)
+                    ],
+                    axis=1,
+                )
+            )
+        gu_v[p] = join(dot_nt(both(*picked).astype(BF16), matrices))
+
+    fields = {14: gu_v[14]}
+    for first, width in ((12, 2), (8, 4), (0, 8)):
+        for p in range(width // 2):
+            row = first + 2 * p
+            matrices = transfer_v[row : row + 2].reshape(LANES, LANES)
+            down = dot_nn(spread(fields[first + width + p], diagonal), matrices)
+            fields[row] = gu_v[row] + down[:COLS]
+            fields[row + 1] = gu_v[row + 1] + down[COLS:]
+    for p in range(LEAVES // 2):
+        matrices = basis_v[2 * p : 2 * p + 2].reshape(LANES, LANES)
+        far = dot_nn(spread(fields[p], diagonal), matrices)
+        out_v[:, 2 * p * LANES : (2 * p + 1) * LANES] = far[:COLS]
+        out_v[:, (2 * p + 1) * LANES : (2 * p + 2) * LANES] = far[COLS:]
+
+    def zero_points(slot):
+        def fill():
+            xr_v[slot] = jnp.zeros(xr_v.shape[1:], BF16)
+
+        return fill
+
+    for device_at, device_core, slot, there, source_slot in point_sends:
+        fill = zero_points(source_slot)
+        if there is not None:
+            pl.when(jnp.logical_not(there))(fill)
+        when(there, lambda: send_points(source_slot, device_at, device_core).wait_recv())
+
+    def arrange(base, mine, theirs):
+        for p in range(LEAVES // 2):
+            a = mine[p].astype(F32)
+            b = theirs[p].astype(F32)
+            xw_v[base + 2 * p] = both(a[:COLS], b[:COLS]).astype(BF16)
+            xw_v[base + 2 * p + 1] = both(a[COLS:], b[COLS:]).astype(BF16)
+
+    arrange(0, xr_v.at[0], xr_v.at[2])
+    arrange(LEAVES, xs_v, xr_v.at[4])
+    arrange(2 * LEAVES, xr_v.at[1], xr_v.at[3])
+
+    for j in range(LEAVES):
+        pltpu.make_async_copy(near_h.at[j], near_v.at[j], near_sem.at[j]).wait()
+
+    def near_leaves(step, carry):
+        for i in range(NEAR_STEP):
+            j = step * NEAR_STEP + i
+            points = jnp.concatenate([xw_v[nid_s[j, s]] for s in range(SLOTS)], axis=1)
+            blocks = jnp.concatenate([near_v[j, s] for s in range(SLOTS)], axis=1)
+            total = dot_nt(points, blocks)
+            yown_v[j] = total[:COLS]
+            ysend_v[j] = total[COLS:]
         return carry
 
-    lax.fori_loop(0, PAIRS, couple, 0)
-
-    pltpu.make_async_copy(ctr_h.at[pl.ds(0, 14)], ctr_v, in_sem.at[10]).wait()
-    pltpu.make_async_copy(ccp_h.at[pl.ds(0, 2)], ccp_v, in_sem.at[11]).wait()
-    for copy in get_coarse:
-        copy.wait()
-    everyone = remote(cr_v, cr_v, csend_sem, crecv_sem, me, other)
-    everyone.wait_send()
-    everyone.wait_recv()
+    lax.fori_loop(0, LEAVES // NEAR_STEP, near_leaves, 0)
+    send_near = remote(ysend_v, yrecv_v, ysend_sem, yrecv_sem, me, other)
+    send_near.start()
+
+    for k, (first, size, to, _, there, source_there) in enumerate(groups):
+        arrived = cr_v.at[pl.ds(first, size)]
+
+        def zero_group():
+            arrived[...] = jnp.zeros((size, COLS, LANES), F32)
+
+        pl.when(jnp.logical_not(source_there))(zero_group)
+        group = remote(arrived, arrived, csend_sem.at[k], crecv_sem.at[k], me, other)
+        when(source_there, group.wait_recv)
     for k in range(3):
         up_v[4 * k + 3] = zero
     for n in range(3):
-        pair = both(meet(cr_v[4 * n], cr_v[4 * n + 1]), meet(cr_v[4 * n + 2], cr_v[4 * n + 3]))
-        upper = join(dot_nt(pair.astype(BF16), ctr_v[2 * n : 2 * n + 2].reshape(LANES, LANES)))
-        matrix = ctr_v[9 + n]
-        up_v[n] = dot_nt(both(upper, upper).astype(BF16), both(matrix, matrix))[:COLS]
+        pairs = [meet(cr_v[4 * n + i], cr_v[4 * n + i + 1]) for i in (0, 2)]
+        children = jnp.concatenate(pairs, axis=1)
+        matrix = rise_v[n]
+        up_v[n] = dot_nt(both(children, children).astype(BF16), both(matrix, matrix))[:COLS]
         pair = meet(cr_v[12 + 2 * n], cr_v[13 + 2 * n])
         matrix = ctr_v[6 + n]
         up_v[4 + n] = dot_nt(both(pair, pair).astype(BF16), both(matrix, matrix))[:COLS]
         up_v[8 + n] = cr_v[18 + n]
 
-    def upper_terms(matrix, at, node_here, base):
+    def upper_rows(at, node_here, base):
         rows = []
         for s in range(3):
             step = clist_s[s, at] - node_here
             row = jnp.where(step == -2, 0, jnp.where(step == 2, 1, 2))
             rows.append(base + jnp.where(s < ccount_s[at], row, 3))
-        pair = meet(up_v[rows[0]], up_v[rows[1]])
-        third = up_v[rows[2]]
-        total = dot_nt(both(pair, pair).astype(BF16), matrix[:, :LANES])
-        total += dot_nt(both(third, third)[:, :RANK].astype(BF16), matrix[:, LANES:])
-        return total
-
-    g6 = upper_terms(ccp_v[1], HALF + quad, quad, 0)
-    g5 = upper_terms(ccp_v[0], duo, duo, 4)
-
-    def pick_child(product, side):
-        return jnp.where(side == 0, product, pltpu.roll(product, RANK, 1))[:, :RANK]
-
-    field = g6.astype(BF16)
-    field = g5 + pick_child(dot_nn(field, ctr_v[13]), lax.rem(duo, 2))
-    field = field.astype(BF16)
+        return meet(up_v[rows[0]], up_v[rows[1]]), up_v[rows[2]]
+
+    pair6, third6 = upper_rows(HALF + quad, quad, 0)
+    pair5, third5 = upper_rows(duo, duo, 4)
+    total = dot_nt(both(pair6, pair5).astype(BF16), both(ccp_v[1, :, :LANES], ccp_v[0, :, :LANES]))
+    total += dot_nt(
+        both(third6, third5)[:, :RANK].astype(BF16), both(ccp_v[1, :, LANES:], ccp_v[0, :, LANES:])
+    )
     matrix = coupling_v[ROWS - 2]
     pair = meet(up_v[8 + fid_s[0, ROWS - 2]], up_v[8 + fid_s[1, ROWS - 2]])
     third = up_v[8 + fid_s[2, ROWS - 2]]
-    g4 = dot_nt(both(pair, pair).astype(BF16), matrix[:, :LANES])
-    g4 += dot_nt(both(third, third)[:, :RANK].astype(BF16), matrix[:, LANES : LANES + RANK])
-    field = g4 + pick_child(dot_nn(field, ctr_v[12]), in_duo)
-    fu_v[14] = gu_v[14] + dot_nn(field.astype(BF16), transfer_v[14])[:COLS]
-    for first, width in ((12, 2), (8, 4), (0, 8)):
-        for p in range(width // 2):
-            pair = fu_v[first + width + p]
-            spread = jnp.where(diagonal, both(pair, pair), 0.0).astype(BF16)
-            row = first + 2 * p
-            down = dot_nn(spread, transfer_v[row : row + 2].reshape(LANES, LANES))
-            fu_v[row] = gu_v[row] + down[:COLS]
-            fu_v[row + 1] = gu_v[row + 1] + down[COLS:]
+    field = dot_nt(both(pair, pair).astype(BF16), matrix[:, :LANES])
+    field += dot_nt(both(third, third)[:, :RANK].astype(BF16), matrix[:, LANES : LANES + RANK])
+    above = join(total)
+    field += dot_nn(both(above, above).astype(BF16), fall_v[...])[:, :RANK]
+    far = dot_nn(field.astype(BF16), reach_v[...])[:COLS]
+
+    for device_at, device_core, slot, there, _ in point_sends:
+        when(there, lambda: send_points(slot, device_at, device_core).wait_send())
+    for slot, device_at, there, _ in side_sends:
+        when(there, lambda: send_side(slot, device_at).wait_send())
+    for k, (first, size, to, _, there, _) in enumerate(groups):
+        left_group = cr_v.at[pl.ds(first, size)]
+        group = remote(left_group, left_group, csend_sem.at[k], crecv_sem.at[k], me, other)
+        when(there, group.wait_send)
     send_near.wait()
-    for p in range(LEAVES // 2):
-        pair = fu_v[p]
-        spread = jnp.where(diagonal, both(pair, pair), 0.0).astype(BF16)
-        far = dot_nn(spread, basis_v[2 * p : 2 * p + 2].reshape(LANES, LANES))
-        for half in range(2):
-            j = 2 * p + half
-            columns = slice(j * LANES, (j + 1) * LANES)
-            out_v[:, columns] += far[half * COLS : (half + 1) * COLS] + yrecv_v[j]
+    for j in range(LEAVES):
+        columns = slice(j * LANES, (j + 1) * LANES)
+        out_v[:, columns] += far[:, columns] + yown_v[j] + yrecv_v[j]
 
 
 def body(
@@ -422,7 +527,7 @@
     dma = pltpu.SemaphoreType.DMA
     return pl.pallas_call(
         kernel,
-        out_shape=jax.ShapeDtypeStruct((COLS, LEAVES * LANES), F32),
+        out_shape=pltpu.VMEM((COLS, LEAVES * LANES), F32),
         in_specs=[pl.BlockSpec(memory_space=pltpu.HBM)] * 14,
         out_specs=pl.BlockSpec(memory_space=pltpu.VMEM),
         scratch_shapes=[
@@ -454,7 +559,10 @@
             pltpu.VMEM((ZERO + 1, COLS, LANES), F32),
             pltpu.VMEM((PAIRS, COLS, LANES), F32),
             pltpu.VMEM((PAIRS, COLS, LANES), F32),
-            pltpu.VMEM((PAIRS, COLS, LANES), F32),
+            pltpu.VMEM((RANK, LEAVES * LANES), BF16),
+            pltpu.VMEM((3, RANK, 2 * LANES), BF16),
+            pltpu.VMEM((LANES, LANES), BF16),
+            pltpu.VMEM((LEAVES, COLS, LANES), F32),
             pltpu.VMEM((LEAVES, COLS, LANES), F32),
             pltpu.VMEM((LEAVES, COLS, LANES), F32),
             dma((13,)),
@@ -464,8 +572,8 @@
             dma((5,)),
             dma((2,)),
             dma((2,)),
-            dma,
-            dma,
+            dma((9,)),
+            dma((9,)),
             dma,
             dma,
         ],

time: 30.1 us -> 19.8 us (0.66)
  the two profiles are of different devices: /device:TPU:1 before, /device:TPU:7 now
where the time goes in v2:
time: 19.8 us; the launch traced here: 19.7 us
  Pallas kernels  19 us (96%)
  local copies, waits for them, and re-layouts  0.63 us (3%)
    pallas_call x1, Pallas kernels, body(): pl.pallas_call(kernel, out_shape=pltpu.VMEM((COLS, LEAVES * LANES), F32),...  19 us
    unnamed x1, local copies, waits for them, and re-layouts  0.63 us

profile of v2, /device:TPU:7, one launch (start us, length us, event | category | flops | bytes accessed | tf_op | source)
XLA Modules:
  0.0 19.7 jit_solution(4117917718217058212)
XLA Ops:
  0.0 19.0 %shard_map.136 = f32[8,2048]{1,0:T(8,128)S(1)} custom-call(f32[8,2048]{1,0:T(8,128)} %rs_h.1, s32[16,128]{1,0:T(8,128)} %bitcast.5, bf16[16,64,128]{2,1,0:T(8,128)(2,1)} %basis_h.1, bf16[15,64,128]{2,1,0:T(8,128)(2,1)} %transfer_h.1, bf16[31,64,512]{2,1,0:T(8,128)(2,1)} %coupling_h.1, s32[8,31]{1,0:T(8,128)} %bitcast.6, s32[1,31]{1,0:T(1,128)} %bitcast.8, ...), custom_call_target="tpu_custom_call" | custom-call | tf_op jit(solution)/shard_map/pallas_call | solution.py:528
  19.0 0.6 %copy.16 = f32[8,2048]{1,0:T(8,128)} copy(f32[8,2048]{1,0:T(8,128)S(1)} %shard_map.136) | data formatting | bytes 131072

commit v3 on v2

--- a/solution.py
+++ b/solution.py
@@ -109,6 +109,8 @@
     crecv_sem,
     ysend_sem,
     yrecv_sem,
+    near_ready,
+    far_ready,
 ):
     me = lax.axis_index("leaf")
     core = lax.axis_index("rhs")
@@ -170,19 +172,19 @@
             device_id_type=MESH,
         )
 
-    peers = 1
-    for device_at, device_core, _, there, _ in point_sends:
-        when(there, lambda: greet(device_at, device_core))
-        if there is not None:
-            peers = peers + jnp.where(there, 1, 0)
+    when(has_right, lambda: greet(right, 1))
+    when(has_left, lambda: greet(left, 1))
+    when(core == 0, lambda: greet(me, 1))
+    near_peers = 1 + 2 * jnp.where(has_right, 1, 0) + 2 * jnp.where(has_left, 1, 0)
+    far_peers = 0
     for _, size, to, _, there, source_there in groups:
 
         def greet_all():
             for i in range(size):
-                greet(to + i, core)
+                greet(to + i, 0)
 
         when(there, greet_all)
-        peers = peers + jnp.where(source_there, size, 0)
+        far_peers = far_peers + 2 * jnp.where(there, size, 0)
     for j in range(4):
         fetch(near_h.at[j], near_v.at[j], near_sem.at[j])
     for n in range(3):
@@ -231,6 +233,40 @@
                 block = jnp.where(chunk == c, found, block)
             blocks.append(block)
         xs_v[j // 2] = both(*blocks).astype(BF16)
+
+    def remote(source, target, send_sem, recv_sem, device_at, device_core):
+        return pltpu.make_async_remote_copy(
+            src_ref=source,
+            dst_ref=target,
+            send_sem=send_sem,
+            recv_sem=recv_sem,
+            device_id=(device_at, device_core),
+            device_id_type=MESH,
+        )
+
+    def send_points(slot, device_at, device_core):
+        return remote(
+            xs_v, xr_v.at[slot], xsend_sem.at[slot], xrecv_sem.at[slot], device_at, device_core
+        )
+
+    def send_side(slot, device_at):
+        return remote(us_v, ur_v.at[slot], usend_sem.at[slot], urecv_sem.at[slot], device_at, core)
+
+    def tell(sem):
+        pl.semaphore_signal(sem, inc=1, device_id=(me, other), device_id_type=MESH)
+
+    def near_gate():
+        pl.semaphore_wait(pltpu.get_barrier_semaphore(), near_peers)
+        tell(near_ready)
+
+    def far_gate():
+        pl.semaphore_wait(pltpu.get_barrier_semaphore(), far_peers)
+        tell(far_ready)
+
+    when(core == 1, near_gate)
+    when(core == 0, lambda: pl.semaphore_wait(near_ready, 1))
+    for device_at, device_core, slot, there, _ in point_sends:
+        when(there, lambda: send_points(slot, device_at, device_core).start())
 
     get_basis.wait()
     get_transfer.wait()
@@ -256,6 +292,9 @@
         first += width
     last = both(up_v[14], jnp.zeros((COLS, LANES), F32)).astype(BF16)
     us_v[7] = last
+    side_sends = ((0, right, has_right, 1), (1, left, has_left, 0))
+    for slot, device_at, there, _ in side_sends:
+        when(there, lambda: send_side(slot, device_at).start())
     root = transfer_v[14]
     cs_v[...] = dot_nt(last, both(root, root))[:COLS].astype(BF16).astype(F32)
     for copy in get_lists:
@@ -289,38 +328,6 @@
     table_v[ZERO] = zero
     xw_v[NEAR_ZERO] = jnp.zeros((2 * COLS, LANES), BF16)
 
-    def remote(source, target, send_sem, recv_sem, device_at, device_core):
-        return pltpu.make_async_remote_copy(
-            src_ref=source,
-            dst_ref=target,
-            send_sem=send_sem,
-            recv_sem=recv_sem,
-            device_id=(device_at, device_core),
-            device_id_type=MESH,
-        )
-
-    def send_points(slot, device_at, device_core):
-        return remote(
-            xs_v, xr_v.at[slot], xsend_sem.at[slot], xrecv_sem.at[slot], device_at, device_core
-        )
-
-    def send_side(slot, device_at):
-        return remote(us_v, ur_v.at[slot], usend_sem.at[slot], urecv_sem.at[slot], device_at, core)
-
-    pl.semaphore_wait(pltpu.get_barrier_semaphore(), peers)
-    side_sends = ((0, right, has_right, 1), (1, left, has_left, 0))
-    for slot, device_at, there, _ in side_sends:
-        when(there, lambda: send_side(slot, device_at).start())
-    for device_at, device_core, slot, there, _ in point_sends:
-        when(there, lambda: send_points(slot, device_at, device_core).start())
-    for k, (first, size, to, place_in, there, _) in enumerate(groups):
-
-        def send_root():
-            for i in range(size):
-                target = cr_v.at[first + place_in]
-                remote(cs_v, target, csend_sem.at[k], crecv_sem.at[k], to + i, core).start()
-
-        when(there, send_root)
     put_near.wait()
     put_far.wait()
 
@@ -361,6 +368,57 @@
     fall_v[:RANK] = dot_nn(quad_matrix[:, :RANK], duo_matrix).astype(BF16)
     fall_v[RANK:] = duo_matrix
 
+    when(core == 0, far_gate)
+    when(core == 1, lambda: pl.semaphore_wait(far_ready, 1))
+    for k, (first, size, to, place_in, there, _) in enumerate(groups):
+
+        def send_root():
+            for i in range(size):
+                target = cr_v.at[first + place_in]
+                remote(cs_v, target, csend_sem.at[k], crecv_sem.at[k], to + i, core).start()
+
+        when(there, send_root)
+
+    def zero_points(slot):
+        def fill():
+            xr_v[slot] = jnp.zeros(xr_v.shape[1:], BF16)
+
+        return fill
+
+    for device_at, device_core, slot, there, source_slot in point_sends:
+        fill = zero_points(source_slot)
+        if there is not None:
+            pl.when(jnp.logical_not(there))(fill)
+        when(there, lambda: send_points(source_slot, device_at, device_core).wait_recv())
+
+    def arrange(base, mine, theirs):
+        for p in range(LEAVES // 2):
+            a = mine[p].astype(F32)
+            b = theirs[p].astype(F32)
+            xw_v[base + 2 * p] = both(a[:COLS], b[:COLS]).astype(BF16)
+            xw_v[base + 2 * p + 1] = both(a[COLS:], b[COLS:]).astype(BF16)
+
+    arrange(0, xr_v.at[0], xr_v.at[2])
+    arrange(LEAVES, xs_v, xr_v.at[4])
+    arrange(2 * LEAVES, xr_v.at[1], xr_v.at[3])
+
+    for j in range(LEAVES):
+        pltpu.make_async_copy(near_h.at[j], near_v.at[j], near_sem.at[j]).wait()
+
+    def near_leaves(step, carry):
+        for i in range(NEAR_STEP):
+            j = step * NEAR_STEP + i
+            points = jnp.concatenate([xw_v[nid_s[j, s]] for s in range(SLOTS)], axis=1)
+            blocks = jnp.concatenate([near_v[j, s] for s in range(SLOTS)], axis=1)
+            total = dot_nt(points, blocks)
+            yown_v[j] = total[:COLS]
+            ysend_v[j] = total[COLS:]
+        return carry
+
+    lax.fori_loop(0, LEAVES // NEAR_STEP, near_leaves, 0)
+    send_near = remote(ysend_v, yrecv_v, ysend_sem, yrecv_sem, me, other)
+    send_near.start()
+
     def zero_side(slot):
         def fill():
             ur_v[slot] = jnp.zeros(ur_v.shape[1:], BF16)
@@ -408,46 +466,6 @@
         far = dot_nn(spread(fields[p], diagonal), matrices)
         out_v[:, 2 * p * LANES : (2 * p + 1) * LANES] = far[:COLS]
         out_v[:, (2 * p + 1) * LANES : (2 * p + 2) * LANES] = far[COLS:]
-
-    def zero_points(slot):
-        def fill():
-            xr_v[slot] = jnp.zeros(xr_v.shape[1:], BF16)
-
-        return fill
-
-    for device_at, device_core, slot, there, source_slot in point_sends:
-        fill = zero_points(source_slot)
-        if there is not None:
-            pl.when(jnp.logical_not(there))(fill)
-        when(there, lambda: send_points(source_slot, device_at, device_core).wait_recv())
-
-    def arrange(base, mine, theirs):
-        for p in range(LEAVES // 2):
-            a = mine[p].astype(F32)
-            b = theirs[p].astype(F32)
-            xw_v[base + 2 * p] = both(a[:COLS], b[:COLS]).astype(BF16)
-            xw_v[base + 2 * p + 1] = both(a[COLS:], b[COLS:]).astype(BF16)
-
-    arrange(0, xr_v.at[0], xr_v.at[2])
-    arrange(LEAVES, xs_v, xr_v.at[4])
-    arrange(2 * LEAVES, xr_v.at[1], xr_v.at[3])
-
-    for j in range(LEAVES):
-        pltpu.make_async_copy(near_h.at[j], near_v.at[j], near_sem.at[j]).wait()
-
-    def near_leaves(step, carry):
-        for i in range(NEAR_STEP):
-            j = step * NEAR_STEP + i
-            points = jnp.concatenate([xw_v[nid_s[j, s]] for s in range(SLOTS)], axis=1)
-            blocks = jnp.concatenate([near_v[j, s] for s in range(SLOTS)], axis=1)
-            total = dot_nt(points, blocks)
-            yown_v[j] = total[:COLS]
-            ysend_v[j] = total[COLS:]
-        return carry
-
-    lax.fori_loop(0, LEAVES // NEAR_STEP, near_leaves, 0)
-    send_near = remote(ysend_v, yrecv_v, ysend_sem, yrecv_sem, me, other)
-    send_near.start()
 
     for k, (first, size, to, _, there, source_there) in enumerate(groups):
         arrived = cr_v.at[pl.ds(first, size)]
@@ -576,6 +594,8 @@
             dma((9,)),
             dma,
             dma,
+            pltpu.SemaphoreType.REGULAR,
+            pltpu.SemaphoreType.REGULAR,
         ],
         compiler_params=pltpu.CompilerParams(
             collective_id=0, has_side_effects=True, vmem_limit_bytes=56 << 20

time: 19.8 us -> 17.8 us (0.90)
  Pallas kernels: 19 us -> 17.1 us
    pallas_call x1, Pallas kernels: 19 us -> 17.1 us  [body(): pl.pallas_call(kernel, out_shape=pltpu.VMEM((COLS, LEAVES * LANES), F32),...]
where the time goes in v3:
time: 17.8 us; the launch traced here: 17.7 us
  Pallas kernels  17.1 us (96%)
  local copies, waits for them, and re-layouts  0.63 us (4%)
    pallas_call x1, Pallas kernels, body(): pl.pallas_call(kernel, out_shape=pltpu.VMEM((COLS, LEAVES * LANES), F32),...  17.1 us
    unnamed x1, local copies, waits for them, and re-layouts  0.63 us

profile of v3, /device:TPU:7, one launch (start us, length us, event | category | flops | bytes accessed | tf_op | source)
XLA Modules:
  0.0 17.7 jit_solution(1638591583069488454)
XLA Ops:
  0.0 17.1 %shard_map.136 = f32[8,2048]{1,0:T(8,128)S(1)} custom-call(f32[8,2048]{1,0:T(8,128)} %rs_h.1, s32[16,128]{1,0:T(8,128)} %bitcast.5, bf16[16,64,128]{2,1,0:T(8,128)(2,1)} %basis_h.1, bf16[15,64,128]{2,1,0:T(8,128)(2,1)} %transfer_h.1, bf16[31,64,512]{2,1,0:T(8,128)(2,1)} %coupling_h.1, s32[8,31]{1,0:T(8,128)} %bitcast.6, s32[1,31]{1,0:T(1,128)} %bitcast.8, ...), custom_call_target="tpu_custom_call" | custom-call | tf_op jit(solution)/shard_map/pallas_call | solution.py:546
  17.1 0.6 %copy.16 = f32[8,2048]{1,0:T(8,128)} copy(f32[8,2048]{1,0:T(8,128)S(1)} %shard_map.136) | data formatting | bytes 131072

commit v4 on v3

v4 whole, which is shorter than its diff:
```python
import jax
import jax.numpy as jnp
from jax import lax
from jax.experimental import pallas as pl
from jax.experimental.pallas import tpu as pltpu
from jax.sharding import PartitionSpec as P

MESH = pl.DeviceIdType.MESH
F32 = jnp.float32
BF16 = jnp.bfloat16

DEVICES = 128
LEAVES = 16
RANK = 64
LANES = 128
COLS = 8
SLOTS = 14
FAR = 8
PAIRS = 15
ROWS = 2 * LEAVES
ZERO = 3 * ROWS
NEAR_ZERO = 3 * LEAVES
COLUMN = 8
HALF = DEVICES // 2
QUARTER = DEVICES // 4


def near_slots(leaf, core):
    at_y = (leaf & 1) + 2 * (leaf >> 2 & 1)
    at_z = (leaf >> 1 & 1) + 2 * (leaf >> 3 & 1)
    touching = 3 * (2 if at_y in (0, 3) else 3) * (2 if at_z in (0, 3) else 3)
    return min(max(touching - core * SLOTS, 0), SLOTS)


def near_kinds(core):
    kinds = {}
    for leaf in range(LEAVES):
        kinds.setdefault(near_slots(leaf, core), []).append(leaf)
    return sorted((slots, leaves) for slots, leaves in kinds.items() if slots)


def dot_nt(left, right):
    return lax.dot_general(left, right, (((1,), (1,)), ((), ())), preferred_element_type=F32)


def dot_nn(left, right):
    return lax.dot_general(left, right, (((1,), (0,)), ((), ())), preferred_element_type=F32)


def wrap(value, size):
    return lax.rem(value + size, size)


def within(value, size):
    return (value >= 0) & (value < size)


def when(flag, do):
    if flag is None:
        do()
    else:
        pl.when(flag)(do)


def kernel(
    rs_h,
    order_h,
    basis_h,
    transfer_h,
    coupling_h,
    flist_h,
    fcount_h,
    ctr_h,
    ccp_h,
    clist_h,
    ccount_h,
    near_h,
    nlist_h,
    ncount_h,
    out_v,
    rs_v,
    order_v,
    basis_v,
    transfer_v,
    coupling_v,
    near_v,
    flist_v,
    fcount_v,
    nlist_v,
    ncount_v,
    ctr_v,
    ccp_v,
    clist_s,
    ccount_s,
    fid_v,
    nid_v,
    fid_s,
    nid_s,
    xs_v,
    us_v,
    xr_v,
    ur_v,
    cs_v,
    cr_v,
    xw_v,
    table_v,
    up_v,
    blank_v,
    spare_v,
    reach_v,
    rise_v,
    climb_v,
    yown_v,
    ysend_v,
    yrecv_v,
    in_sem,
    near_sem,
    send_sem,
    xrecv_sem,
    urecv_sem,
    csend_sem,
    crecv_sem,
    yrecv_sem,
    near_ready,
    far_ready,
):
    me = lax.axis_index("leaf")
    core = lax.axis_index("rhs")
    other = 1 - core
    quad = lax.div(me, 4)
    in_quad = lax.rem(me, 4)
    duo = lax.div(me, 2)
    in_duo = lax.rem(me, 2)
    turn = 1 - 2 * in_duo
    duo_turn = 1 - 2 * lax.rem(duo, 2)
    quad_turn = 1 - 2 * lax.rem(quad, 2)
    quad_from = [wrap(quad + d, QUARTER) for d in (-2, 2, 3 * quad_turn)]
    duo_from = [wrap(duo + d, HALF) for d in (-2, 2, 3 * duo_turn)]
    groups = []
    for n, (send_by, get_by) in enumerate(((2, -2), (-2, 2), (0, 0))):
        for base, size, node, node_turn, nodes, place_in in (
            (0, 4, quad, quad_turn, QUARTER, in_quad),
            (12, 2, duo, duo_turn, HALF, in_duo),
            (18, 1, me, turn, DEVICES, 0),
        ):
            to = node + (send_by if n < 2 else 3 * node_turn)
            source = node + (get_by if n < 2 else 3 * node_turn)
            groups.append(
                (base + size * n, size, size * to, place_in, within(to, nodes), within(source, nodes))
            )
    left = me - 1
    right = me + 1
    has_left = left >= 0
    has_right = right < DEVICES
    column_first = lax.rem(me, COLUMN) == 0
    left_near = has_left & jnp.logical_not(column_first)
    left_late = has_left & column_first
    to_left = (left, has_left, 2, 0, 0)
    to_right = (right, has_right, 0, 2, 1)

    def fetch(source, target, sem):
        copy = pltpu.make_async_copy(source, target, sem)
        copy.start()
        return copy

    get_order = fetch(order_h, order_v, in_sem.at[0])
    get_rs = fetch(rs_h, rs_v, in_sem.at[1])
    def greet(device_at, device_core):
        pl.semaphore_signal(
            pltpu.get_barrier_semaphore(),
            inc=1,
            device_id=(device_at, device_core),
            device_id_type=MESH,
        )

    when(has_right, lambda: greet(right, jnp.where(lax.rem(right, COLUMN) == 0, 0, 1)))
    when(has_left, lambda: greet(left, 1))
    when(core == 0, lambda: greet(me, 1))
    near_peers = 1 + 2 * jnp.where(has_right, 1, 0) + 2 * jnp.where(left_near, 1, 0)
    far_peers = 2 * jnp.where(left_late, 1, 0)
    for _, size, to, _, there, source_there in groups:

        def greet_all():
            for i in range(size):
                greet(to + i, 0)

        when(there, greet_all)
        far_peers = far_peers + 2 * jnp.where(there, size, 0)

    get_basis = fetch(basis_h, basis_v, in_sem.at[2])
    get_transfer = fetch(transfer_h, transfer_v, in_sem.at[3])
    get_lists = [
        fetch(nlist_h, nlist_v, in_sem.at[4]),
        fetch(ncount_h, ncount_v, in_sem.at[5]),
        fetch(flist_h, flist_v, in_sem.at[6]),
        fetch(fcount_h, fcount_v, in_sem.at[7]),
    ]
    for n in range(3):
        fetch(ctr_h.at[pl.ds(2 * quad_from[n], 2)], ctr_v.at[pl.ds(2 * n, 2)], in_sem.at[8])
        fetch(ctr_h.at[pl.ds(duo_from[n], 1)], ctr_v.at[pl.ds(6 + n, 1)], in_sem.at[8])
        fetch(ctr_h.at[pl.ds(HALF + quad_from[n], 1)], ctr_v.at[pl.ds(9 + n, 1)], in_sem.at[8])
    fetch(ctr_h.at[pl.ds(duo, 1)], ctr_v.at[pl.ds(12, 1)], in_sem.at[8])
    fetch(ctr_h.at[pl.ds(HALF + quad, 1)], ctr_v.at[pl.ds(13, 1)], in_sem.at[8])
    fetch(ccp_h.at[pl.ds(duo, 1)], ccp_v.at[pl.ds(0, 1)], in_sem.at[9])
    fetch(ccp_h.at[pl.ds(HALF + quad, 1)], ccp_v.at[pl.ds(1, 1)], in_sem.at[9])


    low = lax.broadcasted_iota(jnp.int32, (COLS, LANES), 1) < RANK
    low4 = lax.broadcasted_iota(jnp.int32, (COLS // 2, LANES), 1) < RANK
    low16 = lax.broadcasted_iota(jnp.int32, (2 * COLS, LANES), 1) < RANK
    top16 = lax.broadcasted_iota(jnp.int32, (2 * COLS, LANES), 0) < COLS
    diagonal = low16 == top16

    def both(first, second):
        return jnp.concatenate([first, second], axis=0)

    def meet(first, second):
        return jnp.where(low, first, second)

    def flip(pair):
        return pltpu.roll(pair, RANK, 1)

    def join(product):
        return jnp.where(low, product[:COLS], product[COLS:])

    get_order.wait()
    get_rs.wait()
    place = order_v[...] - me * (LEAVES * LANES)
    for j in range(0, LEAVES, 2):
        blocks = []
        for i in (j, j + 1):
            here = jnp.broadcast_to(place[i : i + 1], (COLS, LANES))
            chunk = here // LANES
            lane = here % LANES
            block = jnp.take_along_axis(rs_v[:, 0:LANES], lane, axis=1, mode="promise_in_bounds")
            for c in range(1, LEAVES):
                found = jnp.take_along_axis(
                    rs_v[:, c * LANES : (c + 1) * LANES], lane, axis=1, mode="promise_in_bounds"
                )
                block = jnp.where(chunk == c, found, block)
            blocks.append(block)
        xs_v[j // 2] = both(*blocks).astype(BF16)

    def remote(source, target, send_sem, recv_sem, device_at, device_core):
        return pltpu.make_async_remote_copy(
            src_ref=source,
            dst_ref=target,
            send_sem=send_sem,
            recv_sem=recv_sem,
            device_id=(device_at, device_core),
            device_id_type=MESH,
        )

    def send_points(side):
        device_at, _, slot, _, sem = side
        for to_core, step in ((core, 0), (other, 1)):
            remote(
                xs_v, xr_v.at[slot + step], send_sem.at[sem], xrecv_sem.at[slot // 2], device_at, to_core
            ).start()

    def send_pairs(side):
        device_at, _, slot, _, sem = side
        remote(us_v, ur_v.at[slot // 2], send_sem.at[sem], urecv_sem.at[slot // 2], device_at, core).start()

    def tell(sem):
        pl.semaphore_signal(sem, inc=1, device_id=(me, other), device_id_type=MESH)

    def near_gate():
        pl.semaphore_wait(pltpu.get_barrier_semaphore(), near_peers)
        tell(near_ready)

    def far_gate():
        pl.semaphore_wait(pltpu.get_barrier_semaphore(), far_peers)
        tell(far_ready)

    get_coarse = [fetch(clist_h, clist_s, in_sem.at[0]), fetch(ccount_h, ccount_s, in_sem.at[1])]

    blank_v[...] = jnp.zeros(blank_v.shape, F32)
    when(core == 1, near_gate)
    when(core == 0, lambda: pl.semaphore_wait(near_ready, 1))
    remote(xs_v, xr_v.at[4], send_sem.at[2], xrecv_sem.at[2], me, other).start()
    when(has_right, lambda: send_points(to_right))
    when(left_near, lambda: send_points(to_left))

    get_basis.wait()
    get_transfer.wait()
    def fetch_near(at):
        def do():
            for k, (slots, leaves) in enumerate(near_kinds(at)):
                for j in leaves:
                    used = pl.ds(0, slots)
                    fetch(near_h.at[j, used], near_v.at[j, used], near_sem.at[k])

        return do

    for at in range(2):
        when(core == at, fetch_near(at))
    get_coupling = fetch(coupling_h, coupling_v, in_sem.at[10])
    own = ROWS
    for p in range(LEAVES // 2):
        matrices = basis_v[2 * p : 2 * p + 2].reshape(LANES, LANES)
        pair = join(dot_nt(xs_v[p], matrices))
        up_v[p] = pair
        table_v[own + 2 * p] = pair
        table_v[own + 2 * p + 1] = flip(pair)
    first = 0
    for width in (8, 4, 2):
        for p in range(width // 2):
            tile = both(up_v[first + 2 * p], up_v[first + 2 * p + 1]).astype(BF16)
            us_v[first // 2 + p] = tile
            row = first + 2 * p
            matrices = transfer_v[row : row + 2].reshape(LANES, LANES)
            pair = join(dot_nt(tile, matrices))
            at = first + width + p
            up_v[at] = pair
            table_v[own + 2 * at] = pair
            table_v[own + 2 * at + 1] = flip(pair)
        first += width
    last = both(up_v[14], jnp.zeros((COLS, LANES), F32)).astype(BF16)
    us_v[7] = last
    when(has_right, lambda: send_pairs(to_right))
    when(left_near, lambda: send_pairs(to_left))
    root = transfer_v[14]
    mine = dot_nt(last, both(root, root))
    cs_v[...] = jnp.where(low4, mine[: COLS // 2], mine[COLS // 2 : COLS]).astype(BF16).astype(F32)
    for copy in get_lists:
        copy.wait()
    square = lax.broadcasted_iota(jnp.int32, (LEAVES, LEAVES), 0) == lax.broadcasted_iota(
        jnp.int32, (LEAVES, LEAVES), 1
    )
    counts = jnp.broadcast_to(ncount_v[...], (LEAVES, LEAVES))
    counts = jnp.sum(jnp.where(square, counts, 0), axis=1, keepdims=True)
    slot_at = lax.broadcasted_iota(jnp.int32, (LEAVES, SLOTS), 1) + core * SLOTS
    nid_v[...] = jnp.where(slot_at < counts, nlist_v[...] - (me - 1) * LEAVES, NEAR_ZERO)
    node = lax.broadcasted_iota(jnp.int32, (FAR, ROWS - 1), 1)
    slot_at = lax.broadcasted_iota(jnp.int32, (FAR, ROWS - 1), 0)
    entry = flist_v[...]
    row = jnp.zeros_like(entry)
    for height in range(4):
        width = LEAVES >> height
        start = ROWS - 2 * width
        side = entry // width - me + 1
        inside = (node >= start) & (node < start + width)
        row = jnp.where(inside, side * ROWS + start + entry % width, row)
    row = row + jnp.where(slot_at % 2 == 0, 0, 1 - 2 * (row % 2))
    step = entry - me
    root_row = jnp.where(step == -2, 0, jnp.where(step == 2, 1, 2))
    row = jnp.where(node == ROWS - 2, root_row, row)
    live = slot_at < fcount_v[...]
    fid_v[...] = jnp.where(live, row, jnp.where(node == ROWS - 2, 3, ZERO))
    put_near = fetch(nid_v, nid_s, in_sem.at[4])
    put_far = fetch(fid_v, fid_s, in_sem.at[6])
    zero = jnp.zeros((COLS, LANES), F32)
    table_v[ZERO] = zero
    xw_v[NEAR_ZERO] = jnp.zeros((2 * COLS, LANES), BF16)

    def spread(pair, mask):
        return jnp.where(mask, both(pair, pair), 0.0).astype(BF16)

    low128 = lax.broadcasted_iota(jnp.int32, (LANES, LANES), 1) < RANK
    top128 = lax.broadcasted_iota(jnp.int32, (LANES, LANES), 0) < RANK
    diagonal128 = low128 == top128
    low64 = low128[:RANK]

    def compose():
        chains = {14: transfer_v[14].astype(F32)}
        for first, width in ((12, 2), (8, 4), (0, 8)):
            for p in range(width // 2):
                row = first + 2 * p
                matrices = transfer_v[row : row + 2].reshape(LANES, LANES)
                product = dot_nn(spread(chains[first + width + p], diagonal128), matrices)
                chains[row] = product[:RANK]
                chains[row + 1] = product[RANK:]
        for p in range(LEAVES // 2):
            matrices = basis_v[2 * p : 2 * p + 2].reshape(LANES, LANES)
            product = dot_nn(spread(chains[p], diagonal128), matrices).astype(BF16)
            reach_v[:, 2 * p * LANES : (2 * p + 1) * LANES] = product[:RANK]
            reach_v[:, (2 * p + 1) * LANES : (2 * p + 2) * LANES] = product[RANK:]
        pltpu.make_async_copy(ctr_h.at[pl.ds(0, 14)], ctr_v, in_sem.at[8]).wait()
        pltpu.make_async_copy(ccp_h.at[pl.ds(0, 2)], ccp_v, in_sem.at[9]).wait()
        for copy in get_coarse:
            copy.wait()
        for n in range(3):
            matrix = ctr_v[9 + n].astype(F32)
            product = dot_nn(
                spread(matrix, diagonal128), ctr_v[2 * n : 2 * n + 2].reshape(LANES, LANES)
            ).astype(BF16)
            rise_v[n, :, :LANES] = product[:RANK]
            rise_v[n, :, LANES:] = product[RANK:]
        duo_matrix = ctr_v[12].astype(F32)
        duo_matrix = jnp.where(in_duo == 0, duo_matrix, flip(duo_matrix)).astype(BF16)
        quad_matrix = ctr_v[13].astype(F32)
        quad_matrix = jnp.where(lax.rem(duo, 2) == 0, quad_matrix, flip(quad_matrix)).astype(BF16)
        fall = both(dot_nn(quad_matrix[:, :RANK], duo_matrix), duo_matrix.astype(F32)).T[:RANK].astype(BF16)

        def chosen(at, node_here):
            rows = []
            for s in range(3):
                step = clist_s[s, at] - node_here
                row = jnp.where(step == -2, 0, jnp.where(step == 2, 1, 2))
                rows.append(jnp.where(s < ccount_s[at], row, 3))
            return [[jnp.where(row == n, 1.0, 0.0).astype(F32) for n in range(3)] for row in rows]

        for base, width, part, node_here, at, matrices in (
            (0, 2 * LANES, 1, quad, HALF + quad, [rise_v.at[n] for n in range(3)]),
            (6, LANES, 0, duo, duo, [ctr_v.at[6 + n] for n in range(3)]),
        ):
            onto = fall[:, (1 - part) * RANK : (2 - part) * RANK]
            first_two = dot_nn(onto, ccp_v[part, :, :LANES])
            third = dot_nn(onto, ccp_v[part, :, LANES:])
            flags = chosen(at, node_here)
            for n in range(3):
                matrix = matrices[n][...]
                kept = first_two * jnp.where(low64, flags[0][n], flags[1][n])
                product = dot_nn(kept.astype(BF16), both(matrix, matrix))
                product += dot_nn((third * flags[2][n]).astype(BF16), matrix)
                start = base * LANES + n * width
                climb_v[:, start : start + width] = product.astype(BF16)

    early = lax.rem(me, COLUMN) < COLUMN // 2
    when(early, compose)
    when(core == 0, far_gate)
    when(core == 1, lambda: pl.semaphore_wait(far_ready, 1))
    when(left_late, lambda: send_points(to_left))
    for first, size, to, place_in, there, source_there in groups:

        def send_root():
            for i in range(size):
                target = cr_v.at[first + place_in]
                remote(cs_v, target, csend_sem, crecv_sem, to + i, core).start()

        def skip_root():
            fetch(blank_v.at[pl.ds(0, size)], spare_v.at[pl.ds(first, size)], csend_sem)

        def blank_root():
            fetch(blank_v.at[pl.ds(0, size)], cr_v.at[pl.ds(first, size)], crecv_sem)

        when(there, send_root)
        when(jnp.logical_not(there), skip_root)
        when(jnp.logical_not(source_there), blank_root)

    when(left_late, lambda: send_pairs(to_left))
    when(jnp.logical_not(early), compose)
    put_near.wait()
    put_far.wait()


    get_coupling.wait()
    matrix = coupling_v[ROWS - 2, :, : 4 * RANK].astype(F32)
    for n in range(3):
        flags = [jnp.where(fid_s[s, ROWS - 2] == n, 1.0, 0.0).astype(F32) for s in range(3)]
        kept = matrix[:, :LANES] * jnp.where(low64, flags[0], flags[1])
        kept += jnp.where(low64, matrix[:, LANES:] * flags[2], 0.0)
        climb_v[:, (9 + n) * LANES : (10 + n) * LANES] = kept.astype(BF16)

    def arrived(buffer, sem):
        remote(buffer, buffer, send_sem.at[2], sem, me, other).wait_recv()

    for _, there, _, slot, _ in (to_left, to_right):
        landing = xr_v.at[pl.ds(slot, 2)]

        def zero_points():
            landing[...] = jnp.zeros((2,) + xs_v.shape, BF16)

        when(there, lambda: arrived(landing, xrecv_sem.at[slot // 2]))
        when(jnp.logical_not(there), zero_points)
    arrived(xr_v.at[4], xrecv_sem.at[2])

    def arrange(base, mine, theirs):
        for p in range(LEAVES // 2):
            a = mine[p].astype(F32)
            b = theirs[p].astype(F32)
            xw_v[base + 2 * p] = both(a[:COLS], b[:COLS]).astype(BF16)
            xw_v[base + 2 * p + 1] = both(a[COLS:], b[COLS:]).astype(BF16)

    arrange(0, xr_v.at[0], xr_v.at[1])
    arrange(LEAVES, xs_v, xr_v.at[4])
    arrange(2 * LEAVES, xr_v.at[2], xr_v.at[3])

    def near_leaves(at):
        def do():
            for k, (slots, leaves) in enumerate(near_kinds(at)):
                used = near_v.at[pl.ds(0, len(leaves)), pl.ds(0, slots)]
                pltpu.make_async_copy(used, used, near_sem.at[k]).wait()
            for j in range(LEAVES):
                slots = near_slots(j, at)
                if slots:
                    points = jnp.concatenate([xw_v[nid_s[j, s]] for s in range(slots)], axis=1)
                    blocks = jnp.concatenate([near_v[j, s] for s in range(slots)], axis=1)
                    total = dot_nt(points, blocks)
                else:
                    total = jnp.zeros((2 * COLS, LANES), F32)
                yown_v[j] = total[:COLS]
                ysend_v[j] = total[COLS:]

        return do

    for at in range(2):
        when(core == at, near_leaves(at))
    send_near = remote(ysend_v, yrecv_v, send_sem.at[2], yrecv_sem, me, other)
    send_near.start()

    for _, there, _, slot, _ in (to_left, to_right):
        landing = ur_v.at[slot // 2]

        def zero_pairs():
            landing[...] = jnp.zeros(us_v.shape, BF16)

        when(there, lambda: arrived(landing, urecv_sem.at[slot // 2]))
        when(jnp.logical_not(there), zero_pairs)
    for slot, base in ((0, 0), (1, 2 * ROWS)):
        for t in range(8):
            tile = ur_v[slot, t].astype(F32)
            for half in range(2):
                pair = tile[half * COLS : (half + 1) * COLS]
                table_v[base + 4 * t + 2 * half] = pair
                table_v[base + 4 * t + 2 * half + 1] = flip(pair)


    def couple(p):
        matrices = coupling_v[2 * p : 2 * p + 2].reshape(LANES, FAR * RANK)
        picked = []
        for node in (2 * p, 2 * p + 1):
            picked.append(
                jnp.concatenate(
                    [
                        meet(table_v[fid_s[2 * t, node]], table_v[fid_s[2 * t + 1, node]])
                        for t in range(FAR // 2)
                    ],
                    axis=1,
                )
            )
        return join(dot_nt(both(*picked).astype(BF16), matrices))

    fields = {14: couple(14)}
    for first, width in ((12, 2), (8, 4), (0, 8)):
        for p in range(width // 2):
            row = first + 2 * p
            matrices = transfer_v[row : row + 2].reshape(LANES, LANES)
            incoming = [couple(row), couple(row + 1)]
            down = dot_nn(spread(fields[first + width + p], diagonal), matrices)
            fields[row] = incoming[0] + down[:COLS]
            fields[row + 1] = incoming[1] + down[COLS:]
    for p in range(LEAVES // 2):
        matrices = basis_v[2 * p : 2 * p + 2].reshape(LANES, LANES)
        far = dot_nn(spread(fields[p], diagonal), matrices)
        out_v[:, 2 * p * LANES : (2 * p + 1) * LANES] = far[:COLS]
        out_v[:, (2 * p + 1) * LANES : (2 * p + 2) * LANES] = far[COLS:]

    arrived(cr_v, crecv_sem)
    def root_of(slot):
        packed = cr_v[slot]
        turned = flip(packed)
        return both(jnp.where(low4, packed, turned), jnp.where(low4, turned, packed))

    gathered = [meet(root_of(i), root_of(i + 1)) for i in range(0, 18, 2)]
    gathered += [root_of(i) for i in range(18, 21)]
    gathered = jnp.concatenate(gathered, axis=1)
    field = dot_nt(both(gathered, gathered).astype(BF16), climb_v[...])
    far = dot_nn(field.astype(BF16), reach_v[...])[:COLS]

    arrived(yrecv_v, yrecv_sem)

    def left_here(buffer, sem):
        remote(buffer, buffer, sem, yrecv_sem, me, other).wait_send()

    when(has_left, lambda: left_here(xr_v.at[pl.ds(0, 3)], send_sem.at[0]))
    when(has_right, lambda: left_here(xr_v.at[pl.ds(0, 3)], send_sem.at[1]))
    left_here(xr_v.at[pl.ds(0, 3)], send_sem.at[2])
    left_here(cr_v, csend_sem)
    for j in range(LEAVES):
        columns = slice(j * LANES, (j + 1) * LANES)
        out_v[:, columns] += far[:, columns] + yown_v[j] + yrecv_v[j]


def body(
    right_sides,
    point_order,
    leaf_basis,
    transfer,
    coupling,
    far_list,
    far_count,
    coarse_transfer,
    coarse_coupling,
    coarse_list,
    coarse_count,
    near_block,
    near_list,
    near_count,
):
    tile = (2 * COLS, LANES)
    dma = pltpu.SemaphoreType.DMA
    return pl.pallas_call(
        kernel,
        out_shape=pltpu.VMEM((COLS, LEAVES * LANES), F32),
        in_specs=[pl.BlockSpec(memory_space=pltpu.HBM)] * 14,
        out_specs=pl.BlockSpec(memory_space=pltpu.VMEM),
        scratch_shapes=[
            pltpu.VMEM((COLS, LEAVES * LANES), F32),
            pltpu.VMEM((LEAVES, LANES), jnp.int32),
            pltpu.VMEM((LEAVES, RANK, LANES), BF16),
            pltpu.VMEM((LEAVES - 1, RANK, LANES), BF16),
            pltpu.VMEM((ROWS - 1, RANK, FAR * RANK), BF16),
            pltpu.VMEM((LEAVES, SLOTS, LANES, LANES), BF16),
            pltpu.VMEM((FAR, ROWS - 1), jnp.int32),
            pltpu.VMEM((1, ROWS - 1), jnp.int32),
            pltpu.VMEM((LEAVES, SLOTS), jnp.int32),
            pltpu.VMEM((1, LEAVES), jnp.int32),
            pltpu.VMEM((14, RANK, LANES), BF16),
            pltpu.VMEM((2, RANK, 3 * RANK), BF16),
            pltpu.SMEM((3, 96), jnp.int32),
            pltpu.SMEM((96,), jnp.int32),
            pltpu.VMEM((FAR, ROWS - 1), jnp.int32),
            pltpu.VMEM((LEAVES, SLOTS), jnp.int32),
            pltpu.SMEM((FAR, ROWS - 1), jnp.int32),
            pltpu.SMEM((LEAVES, SLOTS), jnp.int32),
            pltpu.VMEM((LEAVES // 2,) + tile, BF16),
            pltpu.VMEM((LEAVES // 2,) + tile, BF16),
            pltpu.VMEM((5, LEAVES // 2) + tile, BF16),
            pltpu.VMEM((2, LEAVES // 2) + tile, BF16),
            pltpu.VMEM((COLS // 2, LANES), F32),
            pltpu.VMEM((21, COLS // 2, LANES), F32),
            pltpu.VMEM((3 * LEAVES + 1,) + tile, BF16),
            pltpu.VMEM((ZERO + 1, COLS, LANES), F32),
            pltpu.VMEM((PAIRS, COLS, LANES), F32),
            pltpu.VMEM((4, COLS // 2, LANES), F32),
            pltpu.VMEM((21, COLS // 2, LANES), F32),
            pltpu.VMEM((RANK, LEAVES * LANES), BF16),
            pltpu.VMEM((3, RANK, 2 * LANES), BF16),
            pltpu.VMEM((RANK, 12 * LANES), BF16),
            pltpu.VMEM((LEAVES, COLS, LANES), F32),
            pltpu.VMEM((LEAVES, COLS, LANES), F32),
            pltpu.VMEM((LEAVES, COLS, LANES), F32),
            dma((11,)),
            dma((2,)),
            dma((3,)),
            dma((3,)),
            dma((2,)),
            dma,
            dma,
            dma,
            pltpu.SemaphoreType.REGULAR,
            pltpu.SemaphoreType.REGULAR,
        ],
        compiler_params=pltpu.CompilerParams(
            collective_id=0, has_side_effects=True, vmem_limit_bytes=56 << 20
        ),
    )(
        right_sides,
        point_order.reshape(LEAVES, LANES),
        leaf_basis,
        transfer,
        coupling,
        far_list.T,
        far_count.reshape(1, ROWS - 1),
        coarse_transfer,
        coarse_coupling,
        coarse_list.T,
        coarse_count,
        near_block,
        near_list,
        near_count.reshape(1, LEAVES),
    )


def solution(mesh):
    return jax.shard_map(
        body,
        mesh=mesh,
        in_specs=(
            P("rhs", "leaf"),
            P("leaf"),
            P("leaf", None, None),
            P("leaf", None, None),
            P("leaf", None, None),
            P("leaf", None),
            P("leaf"),
            P(),
            P(),
            P(),
            P(),
            P("leaf", "rhs", None, None),
            P("leaf", "rhs"),
            P("leaf"),
        ),
        out_specs=P("rhs", "leaf"),
        check_vma=False,
    )
```

time: 17.8 us -> 16.4 us (0.921)
  Pallas kernels: 17.1 us -> 15.6 us
    pallas_call x1, Pallas kernels: 17.1 us -> 15.6 us  [body(): pl.pallas_call(kernel, out_shape=pltpu.VMEM((COLS, LEAVES * LANES), F32),...]
where the time goes in v4:
time: 16.4 us; the launch traced here: 16.2 us
  Pallas kernels  15.6 us (95%)
  local copies, waits for them, and re-layouts  0.63 us (4%)
    pallas_call x1, Pallas kernels, body(): pl.pallas_call(kernel, out_shape=pltpu.VMEM((COLS, LEAVES * LANES), F32),...  15.6 us
    unnamed x1, local copies, waits for them, and re-layouts  0.63 us

profile of v4, /device:TPU:7, one launch (start us, length us, event | category | flops | bytes accessed | tf_op | source)
XLA Modules:
  0.0 16.2 jit_solution(16798393102943109963)
XLA Ops:
  0.0 15.6 %shard_map.136 = f32[8,2048]{1,0:T(8,128)S(1)} custom-call(f32[8,2048]{1,0:T(8,128)} %rs_h.1, s32[16,128]{1,0:T(8,128)} %bitcast.5, bf16[16,64,128]{2,1,0:T(8,128)(2,1)} %basis_h.1, bf16[15,64,128]{2,1,0:T(8,128)(2,1)} %transfer_h.1, bf16[31,64,512]{2,1,0:T(8,128)(2,1)} %coupling_h.1, s32[8,31]{1,0:T(8,128)} %bitcast.6, s32[1,31]{1,0:T(1,128)} %bitcast.8, ...), custom_call_target="tpu_custom_call" | custom-call | tf_op jit(solution)/shard_map/pallas_call | solution.py:594
  15.6 0.6 %copy.16 = f32[8,2048]{1,0:T(8,128)} copy(f32[8,2048]{1,0:T(8,128)S(1)} %shard_map.136) | data formatting | bytes 131072

commit v5 on v4

--- a/solution.py
+++ b/solution.py
@@ -25,11 +25,11 @@
 QUARTER = DEVICES // 4
 
 
-def near_slots(leaf, core):
+def near_slots(leaf, core, slabs=3):
     at_y = (leaf & 1) + 2 * (leaf >> 2 & 1)
     at_z = (leaf >> 1 & 1) + 2 * (leaf >> 3 & 1)
-    touching = 3 * (2 if at_y in (0, 3) else 3) * (2 if at_z in (0, 3) else 3)
-    return min(max(touching - core * SLOTS, 0), SLOTS)
+    touching = (2 if at_y in (0, 3) else 3) * (2 if at_z in (0, 3) else 3)
+    return min(max(3 * touching - core * SLOTS, 0), SLOTS, slabs * touching)
 
 
 def near_kinds(core):
@@ -53,6 +53,10 @@
 
 def within(value, size):
     return (value >= 0) & (value < size)
+
+
+def starts_first(device):
+    return lax.rem(device + DEVICES, COLUMN) == 0
 
 
 def when(flag, do):
@@ -96,6 +100,8 @@
     nid_v,
     fid_s,
     nid_s,
+    late_v,
+    late_s,
     xs_v,
     us_v,
     xr_v,
@@ -155,6 +161,8 @@
     column_first = lax.rem(me, COLUMN) == 0
     left_near = has_left & jnp.logical_not(column_first)
     left_late = has_left & column_first
+    right_late = has_right & (lax.rem(right, COLUMN) == 0)
+    late = left_late | right_late
     to_left = (left, has_left, 2, 0, 0)
     to_right = (right, has_right, 0, 2, 1)
 
@@ -164,7 +172,9 @@
         return copy
 
     get_order = fetch(order_h, order_v, in_sem.at[0])
-    get_rs = fetch(rs_h, rs_v, in_sem.at[1])
+    for part in range(4):
+        columns = pl.ds(part * (LEAVES * LANES // 4), LEAVES * LANES // 4)
+        fetch(rs_h.at[:, columns], rs_v.at[:, columns], in_sem.at[1])
     def greet(device_at, device_core):
         pl.semaphore_signal(
             pltpu.get_barrier_semaphore(),
@@ -182,10 +192,12 @@
 
         def greet_all():
             for i in range(size):
-                greet(to + i, 0)
+                greet(to + i, jnp.where(starts_first(me), 1, 0))
 
         when(there, greet_all)
-        far_peers = far_peers + 2 * jnp.where(there, size, 0)
+        first_ones = jnp.where(starts_first(to), 1, 0)
+        near_peers = near_peers + 2 * jnp.where(there, first_ones, 0)
+        far_peers = far_peers + 2 * jnp.where(there, size - first_ones, 0)
 
     get_basis = fetch(basis_h, basis_v, in_sem.at[2])
     get_transfer = fetch(transfer_h, transfer_v, in_sem.at[3])
@@ -224,7 +236,7 @@
         return jnp.where(low, product[:COLS], product[COLS:])
 
     get_order.wait()
-    get_rs.wait()
+    pltpu.make_async_copy(rs_h, rs_v, in_sem.at[1]).wait()
     place = order_v[...] - me * (LEAVES * LANES)
     for j in range(0, LEAVES, 2):
         blocks = []
@@ -261,6 +273,28 @@
     def send_pairs(side):
         device_at, _, slot, _, sem = side
         remote(us_v, ur_v.at[slot // 2], send_sem.at[sem], urecv_sem.at[slot // 2], device_at, core).start()
+
+    def send_roots(to_first):
+        for first, size, to, place_in, there, source_there in groups:
+
+            def send_root(i):
+                target = cr_v.at[first + place_in]
+                return lambda: remote(cs_v, target, csend_sem, crecv_sem, to + i, core).start()
+
+            def skip_root():
+                fetch(blank_v.at[pl.ds(0, size)], spare_v.at[pl.ds(first, size)], csend_sem)
+
+            def blank_root():
+                fetch(blank_v.at[pl.ds(0, size)], cr_v.at[pl.ds(first, size)], crecv_sem)
+
+            if to_first:
+                when(there & starts_first(to), send_root(0))
+                when(jnp.logical_not(there), skip_root)
+                when(jnp.logical_not(source_there), blank_root)
+            else:
+                when(there & jnp.logical_not(starts_first(to)), send_root(0))
+                for i in range(1, size):
+                    when(there, send_root(i))
 
     def tell(sem):
         pl.semaphore_signal(sem, inc=1, device_id=(me, other), device_id_type=MESH)
@@ -318,11 +352,13 @@
         first += width
     last = both(up_v[14], jnp.zeros((COLS, LANES), F32)).astype(BF16)
     us_v[7] = last
-    when(has_right, lambda: send_pairs(to_right))
-    when(left_near, lambda: send_pairs(to_left))
     root = transfer_v[14]
     mine = dot_nt(last, both(root, root))
     cs_v[...] = jnp.where(low4, mine[: COLS // 2], mine[COLS // 2 : COLS]).astype(BF16).astype(F32)
+    send_roots(True)
+    when(has_right, lambda: send_pairs(to_right))
+    when(left_near, lambda: send_pairs(to_left))
+
     for copy in get_lists:
         copy.wait()
     square = lax.broadcasted_iota(jnp.int32, (LEAVES, LEAVES), 0) == lax.broadcasted_iota(
@@ -331,7 +367,27 @@
     counts = jnp.broadcast_to(ncount_v[...], (LEAVES, LEAVES))
     counts = jnp.sum(jnp.where(square, counts, 0), axis=1, keepdims=True)
     slot_at = lax.broadcasted_iota(jnp.int32, (LEAVES, SLOTS), 1) + core * SLOTS
-    nid_v[...] = jnp.where(slot_at < counts, nlist_v[...] - (me - 1) * LEAVES, NEAR_ZERO)
+    near_row = jnp.where(slot_at < counts, nlist_v[...] - (me - 1) * LEAVES, NEAR_ZERO)
+    nid_v[...] = near_row
+
+    def list_late():
+        first_row = jnp.where(left_late, 0, 2 * LEAVES)
+        hits = jnp.where((near_row >= first_row) & (near_row < first_row + LEAVES), 1, 0)
+        column = lax.broadcasted_iota(jnp.int32, (LEAVES, LEAVES), 1)
+        place_at = jnp.zeros((LEAVES, LEAVES), jnp.int32)
+        slots = jnp.zeros((LEAVES, LEAVES), jnp.int32)
+        rows = jnp.full((LEAVES, LEAVES), NEAR_ZERO, jnp.int32)
+        for s in range(SLOTS):
+            hit = jnp.broadcast_to(hits[:, s : s + 1], (LEAVES, LEAVES))
+            here = (column == place_at) & (hit == 1)
+            slots = jnp.where(here, s, slots)
+            rows = jnp.where(here, jnp.broadcast_to(near_row[:, s : s + 1], (LEAVES, LEAVES)), rows)
+            place_at = place_at + hit
+        late_v[:LEAVES] = slots
+        late_v[LEAVES:] = rows
+        fetch(late_v, late_s, in_sem.at[5])
+
+    when(late, list_late)
     node = lax.broadcasted_iota(jnp.int32, (FAR, ROWS - 1), 1)
     slot_at = lax.broadcasted_iota(jnp.int32, (FAR, ROWS - 1), 0)
     entry = flist_v[...]
@@ -422,23 +478,7 @@
     when(core == 0, far_gate)
     when(core == 1, lambda: pl.semaphore_wait(far_ready, 1))
     when(left_late, lambda: send_points(to_left))
-    for first, size, to, place_in, there, source_there in groups:
-
-        def send_root():
-            for i in range(size):
-                target = cr_v.at[first + place_in]
-                remote(cs_v, target, csend_sem, crecv_sem, to + i, core).start()
-
-        def skip_root():
-            fetch(blank_v.at[pl.ds(0, size)], spare_v.at[pl.ds(first, size)], csend_sem)
-
-        def blank_root():
-            fetch(blank_v.at[pl.ds(0, size)], cr_v.at[pl.ds(first, size)], crecv_sem)
-
-        when(there, send_root)
-        when(jnp.logical_not(there), skip_root)
-        when(jnp.logical_not(source_there), blank_root)
-
+    send_roots(False)
     when(left_late, lambda: send_pairs(to_left))
     when(jnp.logical_not(early), compose)
     put_near.wait()
@@ -456,14 +496,7 @@
     def arrived(buffer, sem):
         remote(buffer, buffer, send_sem.at[2], sem, me, other).wait_recv()
 
-    for _, there, _, slot, _ in (to_left, to_right):
-        landing = xr_v.at[pl.ds(slot, 2)]
-
-        def zero_points():
-            landing[...] = jnp.zeros((2,) + xs_v.shape, BF16)
-
-        when(there, lambda: arrived(landing, xrecv_sem.at[slot // 2]))
-        when(jnp.logical_not(there), zero_points)
+    sides = ((to_left, left_late, 0), (to_right, right_late, 2 * LEAVES))
     arrived(xr_v.at[4], xrecv_sem.at[2])
 
     def arrange(base, mine, theirs):
@@ -473,9 +506,20 @@
             xw_v[base + 2 * p] = both(a[:COLS], b[:COLS]).astype(BF16)
             xw_v[base + 2 * p + 1] = both(a[COLS:], b[COLS:]).astype(BF16)
 
-    arrange(0, xr_v.at[0], xr_v.at[1])
     arrange(LEAVES, xs_v, xr_v.at[4])
-    arrange(2 * LEAVES, xr_v.at[2], xr_v.at[3])
+
+    def take_side(side, base):
+        slot = side[3]
+        arrived(xr_v.at[pl.ds(slot, 2)], xrecv_sem.at[slot // 2])
+        arrange(base, xr_v.at[slot], xr_v.at[slot + 1])
+
+    def no_side(base):
+        xw_v[base : base + LEAVES] = jnp.zeros((LEAVES, 2 * COLS, LANES), BF16)
+
+    for side, side_late, base in sides:
+        now = side[1] & jnp.logical_not(side_late)
+        when(now, lambda: take_side(side, base))
+        when(jnp.logical_not(now), lambda: no_side(base))
 
     def near_leaves(at):
         def do():
@@ -497,6 +541,25 @@
 
     for at in range(2):
         when(core == at, near_leaves(at))
+    for side, side_late, base in sides:
+        when(side_late, lambda: take_side(side, base))
+
+    def late_leaves(at):
+        def do():
+            pltpu.make_async_copy(late_v, late_s, in_sem.at[5]).wait()
+            for j in range(LEAVES):
+                slots = near_slots(j, at, 1)
+                if slots:
+                    points = [xw_v[late_s[LEAVES + j, t]] for t in range(slots)]
+                    blocks = [near_v[j, late_s[j, t]] for t in range(slots)]
+                    total = dot_nt(jnp.concatenate(points, axis=1), jnp.concatenate(blocks, axis=1))
+                    yown_v[j] += total[:COLS]
+                    ysend_v[j] += total[COLS:]
+
+        return do
+
+    for at in range(2):
+        when(late & (core == at), late_leaves(at))
     send_near = remote(ysend_v, yrecv_v, send_sem.at[2], yrecv_sem, me, other)
     send_near.start()
 
@@ -615,6 +678,8 @@
             pltpu.VMEM((LEAVES, SLOTS), jnp.int32),
             pltpu.SMEM((FAR, ROWS - 1), jnp.int32),
             pltpu.SMEM((LEAVES, SLOTS), jnp.int32),
+            pltpu.VMEM((2 * LEAVES, LEAVES), jnp.int32),
+            pltpu.SMEM((2 * LEAVES, LEAVES), jnp.int32),
             pltpu.VMEM((LEAVES // 2,) + tile, BF16),
             pltpu.VMEM((LEAVES // 2,) + tile, BF16),
             pltpu.VMEM((5, LEAVES // 2) + tile, BF16),

time: 16.4 us -> 16.1 us (0.982)
  Pallas kernels: 15.6 us -> 15.4 us
    pallas_call x1, Pallas kernels: 15.6 us -> 15.4 us  [body(): pl.pallas_call(kernel, out_shape=pltpu.VMEM((COLS, LEAVES * LANES), F32),...]
where the time goes in v5:
time: 16.1 us; the launch traced here: 16 us
  Pallas kernels  15.4 us (96%)
  local copies, waits for them, and re-layouts  0.63 us (4%)
    pallas_call x1, Pallas kernels, body(): pl.pallas_call(kernel, out_shape=pltpu.VMEM((COLS, LEAVES * LANES), F32),...  15.4 us
    unnamed x1, local copies, waits for them, and re-layouts  0.63 us

profile of v5, /device:TPU:7, one launch (start us, length us, event | category | flops | bytes accessed | tf_op | source)
XLA Modules:
  0.0 16.0 jit_solution(13945333653946720897)
XLA Ops:
  0.0 15.4 %shard_map.136 = f32[8,2048]{1,0:T(8,128)S(1)} custom-call(f32[8,2048]{1,0:T(8,128)} %rs_h.1, s32[16,128]{1,0:T(8,128)} %bitcast.5, bf16[16,64,128]{2,1,0:T(8,128)(2,1)} %basis_h.1, bf16[15,64,128]{2,1,0:T(8,128)(2,1)} %transfer_h.1, bf16[31,64,512]{2,1,0:T(8,128)(2,1)} %coupling_h.1, s32[8,31]{1,0:T(8,128)} %bitcast.6, s32[1,31]{1,0:T(1,128)} %bitcast.8, ...), custom_call_target="tpu_custom_call" | custom-call | tf_op jit(solution)/shard_map/pallas_call | solution.py:657
  15.4 0.6 %copy.16 = f32[8,2048]{1,0:T(8,128)} copy(f32[8,2048]{1,0:T(8,128)S(1)} %shard_map.136) | data formatting | bytes 131072

commit v6 on v5

--- a/solution.py
+++ b/solution.py
@@ -21,6 +21,7 @@
 ZERO = 3 * ROWS
 NEAR_ZERO = 3 * LEAVES
 COLUMN = 8
+PLANE = 32
 HALF = DEVICES // 2
 QUARTER = DEVICES // 4
 
@@ -127,6 +128,7 @@
     csend_sem,
     crecv_sem,
     yrecv_sem,
+    ahead_sem,
     near_ready,
     far_ready,
 ):
@@ -163,6 +165,8 @@
     left_late = has_left & column_first
     right_late = has_right & (lax.rem(right, COLUMN) == 0)
     late = left_late | right_late
+    far_left = left_late & (lax.rem(me, PLANE) == 0)
+    far_right = right_late & (lax.rem(right, PLANE) == 0)
     to_left = (left, has_left, 2, 0, 0)
     to_right = (right, has_right, 0, 2, 1)
 
@@ -263,12 +267,12 @@
             device_id_type=MESH,
         )
 
-    def send_points(side):
+    def send_points(side, steps=(0, 1), sem_there=None):
         device_at, _, slot, _, sem = side
-        for to_core, step in ((core, 0), (other, 1)):
-            remote(
-                xs_v, xr_v.at[slot + step], send_sem.at[sem], xrecv_sem.at[slot // 2], device_at, to_core
-            ).start()
+        sem_there = xrecv_sem.at[slot // 2] if sem_there is None else sem_there
+        for step in steps:
+            to_core = other if step else core
+            remote(xs_v, xr_v.at[slot + step], send_sem.at[sem], sem_there, device_at, to_core).start()
 
     def send_pairs(side):
         device_at, _, slot, _, sem = side
@@ -313,7 +317,8 @@
     when(core == 1, near_gate)
     when(core == 0, lambda: pl.semaphore_wait(near_ready, 1))
     remote(xs_v, xr_v.at[4], send_sem.at[2], xrecv_sem.at[2], me, other).start()
-    when(has_right, lambda: send_points(to_right))
+    when(far_right & (core == 1), lambda: send_points(to_right, (0,), ahead_sem))
+    when(has_right & jnp.logical_not(far_right & (core == 1)), lambda: send_points(to_right))
     when(left_near, lambda: send_points(to_left))
 
     get_basis.wait()
@@ -475,29 +480,10 @@
 
     early = lax.rem(me, COLUMN) < COLUMN // 2
     when(early, compose)
-    when(core == 0, far_gate)
-    when(core == 1, lambda: pl.semaphore_wait(far_ready, 1))
-    when(left_late, lambda: send_points(to_left))
-    send_roots(False)
-    when(left_late, lambda: send_pairs(to_left))
-    when(jnp.logical_not(early), compose)
-    put_near.wait()
-    put_far.wait()
-
-
-    get_coupling.wait()
-    matrix = coupling_v[ROWS - 2, :, : 4 * RANK].astype(F32)
-    for n in range(3):
-        flags = [jnp.where(fid_s[s, ROWS - 2] == n, 1.0, 0.0).astype(F32) for s in range(3)]
-        kept = matrix[:, :LANES] * jnp.where(low64, flags[0], flags[1])
-        kept += jnp.where(low64, matrix[:, LANES:] * flags[2], 0.0)
-        climb_v[:, (9 + n) * LANES : (10 + n) * LANES] = kept.astype(BF16)
-
     def arrived(buffer, sem):
         remote(buffer, buffer, send_sem.at[2], sem, me, other).wait_recv()
 
     sides = ((to_left, left_late, 0), (to_right, right_late, 2 * LEAVES))
-    arrived(xr_v.at[4], xrecv_sem.at[2])
 
     def arrange(base, mine, theirs):
         for p in range(LEAVES // 2):
@@ -506,8 +492,6 @@
             xw_v[base + 2 * p] = both(a[:COLS], b[:COLS]).astype(BF16)
             xw_v[base + 2 * p + 1] = both(a[COLS:], b[COLS:]).astype(BF16)
 
-    arrange(LEAVES, xs_v, xr_v.at[4])
-
     def take_side(side, base):
         slot = side[3]
         arrived(xr_v.at[pl.ds(slot, 2)], xrecv_sem.at[slot // 2])
@@ -515,11 +499,6 @@
 
     def no_side(base):
         xw_v[base : base + LEAVES] = jnp.zeros((LEAVES, 2 * COLS, LANES), BF16)
-
-    for side, side_late, base in sides:
-        now = side[1] & jnp.logical_not(side_late)
-        when(now, lambda: take_side(side, base))
-        when(jnp.logical_not(now), lambda: no_side(base))
 
     def near_leaves(at):
         def do():
@@ -539,10 +518,52 @@
 
         return do
 
-    for at in range(2):
-        when(core == at, near_leaves(at))
-    for side, side_late, base in sides:
-        when(side_late, lambda: take_side(side, base))
+    def near_first():
+        put_near.wait()
+        arrived(xr_v.at[4], xrecv_sem.at[2])
+
+        arrange(LEAVES, xs_v, xr_v.at[4])
+
+        for side, side_late, base in sides:
+            now = side[1] & jnp.logical_not(side_late)
+            when(now, lambda: take_side(side, base))
+            when(jnp.logical_not(now), lambda: no_side(base))
+
+        for at in range(2):
+            when(core == at, near_leaves(at))
+
+    when(far_left, near_first)
+    when(core == 0, far_gate)
+    when(core == 1, lambda: pl.semaphore_wait(far_ready, 1))
+    when(left_late, lambda: send_points(to_left))
+    send_roots(False)
+    when(left_late, lambda: send_pairs(to_left))
+    when(jnp.logical_not(early), compose)
+    put_far.wait()
+
+
+    get_coupling.wait()
+    matrix = coupling_v[ROWS - 2, :, : 4 * RANK].astype(F32)
+    for n in range(3):
+        flags = [jnp.where(fid_s[s, ROWS - 2] == n, 1.0, 0.0).astype(F32) for s in range(3)]
+        kept = matrix[:, :LANES] * jnp.where(low64, flags[0], flags[1])
+        kept += jnp.where(low64, matrix[:, LANES:] * flags[2], 0.0)
+        climb_v[:, (9 + n) * LANES : (10 + n) * LANES] = kept.astype(BF16)
+
+    when(jnp.logical_not(far_left), near_first)
+    def take_far():
+        slot = to_left[3]
+        arrived(xr_v.at[slot], ahead_sem)
+        remote(
+            xr_v.at[slot], xr_v.at[slot + 1], send_sem.at[2], xrecv_sem.at[slot // 2], me, other
+        ).start()
+        arrived(xr_v.at[slot + 1], xrecv_sem.at[slot // 2])
+        arrange(0, xr_v.at[slot], xr_v.at[slot + 1])
+
+    far_one = far_left & (core == 1)
+    when(far_one, take_far)
+    when(left_late & jnp.logical_not(far_one), lambda: take_side(to_left, 0))
+    when(right_late, lambda: take_side(to_right, 2 * LEAVES))
 
     def late_leaves(at):
         def do():
@@ -628,8 +649,12 @@
         remote(buffer, buffer, sem, yrecv_sem, me, other).wait_send()
 
     when(has_left, lambda: left_here(xr_v.at[pl.ds(0, 3)], send_sem.at[0]))
-    when(has_right, lambda: left_here(xr_v.at[pl.ds(0, 3)], send_sem.at[1]))
-    left_here(xr_v.at[pl.ds(0, 3)], send_sem.at[2])
+    for flag, there, sem, units in (
+        (far_right & (core == 1), has_right, send_sem.at[1], 2),
+        (far_one, True, send_sem.at[2], 4),
+    ):
+        when(flag, lambda: left_here(xr_v.at[pl.ds(0, units)], sem))
+        when(there & jnp.logical_not(flag), lambda: left_here(xr_v.at[pl.ds(0, 3)], sem))
     left_here(cr_v, csend_sem)
     for j in range(LEAVES):
         columns = slice(j * LANES, (j + 1) * LANES)
@@ -705,6 +730,7 @@
             dma,
             dma,
             dma,
+            dma,
             pltpu.SemaphoreType.REGULAR,
             pltpu.SemaphoreType.REGULAR,
         ],

time: 16.1 us -> 16.1 us (level)
  no operation moved by 1% of the time
where the time goes in v6:
time: 16.1 us; the launch traced here: 16 us
  Pallas kernels  15.4 us (96%)
  local copies, waits for them, and re-layouts  0.63 us (4%)
    pallas_call x1, Pallas kernels, body(): pl.pallas_call(kernel, out_shape=pltpu.VMEM((COLS, LEAVES * LANES), F32),...  15.4 us
    unnamed x1, local copies, waits for them, and re-layouts  0.63 us

profile of v6, /device:TPU:7, one launch (start us, length us, event | category | flops | bytes accessed | tf_op | source)
XLA Modules:
  0.0 16.0 jit_solution(17549007382376516712)
XLA Ops:
  0.0 15.4 %shard_map.136 = f32[8,2048]{1,0:T(8,128)S(1)} custom-call(f32[8,2048]{1,0:T(8,128)} %rs_h.1, s32[16,128]{1,0:T(8,128)} %bitcast.5, bf16[16,64,128]{2,1,0:T(8,128)(2,1)} %basis_h.1, bf16[15,64,128]{2,1,0:T(8,128)(2,1)} %transfer_h.1, bf16[31,64,512]{2,1,0:T(8,128)(2,1)} %coupling_h.1, s32[8,31]{1,0:T(8,128)} %bitcast.6, s32[1,31]{1,0:T(1,128)} %bitcast.8, ...), custom_call_target="tpu_custom_call" | custom-call | tf_op jit(solution)/shard_map/pallas_call | solution.py:682
  15.4 0.6 %copy.16 = f32[8,2048]{1,0:T(8,128)} copy(f32[8,2048]{1,0:T(8,128)S(1)} %shard_map.136) | data formatting | bytes 131072

commit v7 on v6

--- a/solution.py
+++ b/solution.py
@@ -129,8 +129,7 @@
     crecv_sem,
     yrecv_sem,
     ahead_sem,
-    near_ready,
-    far_ready,
+    ready,
 ):
     me = lax.axis_index("leaf")
     core = lax.axis_index("rhs")
@@ -211,14 +210,6 @@
         fetch(flist_h, flist_v, in_sem.at[6]),
         fetch(fcount_h, fcount_v, in_sem.at[7]),
     ]
-    for n in range(3):
-        fetch(ctr_h.at[pl.ds(2 * quad_from[n], 2)], ctr_v.at[pl.ds(2 * n, 2)], in_sem.at[8])
-        fetch(ctr_h.at[pl.ds(duo_from[n], 1)], ctr_v.at[pl.ds(6 + n, 1)], in_sem.at[8])
-        fetch(ctr_h.at[pl.ds(HALF + quad_from[n], 1)], ctr_v.at[pl.ds(9 + n, 1)], in_sem.at[8])
-    fetch(ctr_h.at[pl.ds(duo, 1)], ctr_v.at[pl.ds(12, 1)], in_sem.at[8])
-    fetch(ctr_h.at[pl.ds(HALF + quad, 1)], ctr_v.at[pl.ds(13, 1)], in_sem.at[8])
-    fetch(ccp_h.at[pl.ds(duo, 1)], ccp_v.at[pl.ds(0, 1)], in_sem.at[9])
-    fetch(ccp_h.at[pl.ds(HALF + quad, 1)], ccp_v.at[pl.ds(1, 1)], in_sem.at[9])
 
 
     low = lax.broadcasted_iota(jnp.int32, (COLS, LANES), 1) < RANK
@@ -305,17 +296,17 @@
 
     def near_gate():
         pl.semaphore_wait(pltpu.get_barrier_semaphore(), near_peers)
-        tell(near_ready)
+        tell(ready)
 
     def far_gate():
         pl.semaphore_wait(pltpu.get_barrier_semaphore(), far_peers)
-        tell(far_ready)
+        tell(ready)
 
     get_coarse = [fetch(clist_h, clist_s, in_sem.at[0]), fetch(ccount_h, ccount_s, in_sem.at[1])]
 
     blank_v[...] = jnp.zeros(blank_v.shape, F32)
     when(core == 1, near_gate)
-    when(core == 0, lambda: pl.semaphore_wait(near_ready, 1))
+    when(core == 0, lambda: pl.semaphore_wait(ready, 1))
     remote(xs_v, xr_v.at[4], send_sem.at[2], xrecv_sem.at[2], me, other).start()
     when(far_right & (core == 1), lambda: send_points(to_right, (0,), ahead_sem))
     when(has_right & jnp.logical_not(far_right & (core == 1)), lambda: send_points(to_right))
@@ -323,6 +314,14 @@
 
     get_basis.wait()
     get_transfer.wait()
+    for n in range(3):
+        fetch(ctr_h.at[pl.ds(2 * quad_from[n], 2)], ctr_v.at[pl.ds(2 * n, 2)], in_sem.at[2])
+        fetch(ctr_h.at[pl.ds(duo_from[n], 1)], ctr_v.at[pl.ds(6 + n, 1)], in_sem.at[2])
+        fetch(ctr_h.at[pl.ds(HALF + quad_from[n], 1)], ctr_v.at[pl.ds(9 + n, 1)], in_sem.at[2])
+    fetch(ctr_h.at[pl.ds(duo, 1)], ctr_v.at[pl.ds(12, 1)], in_sem.at[2])
+    fetch(ctr_h.at[pl.ds(HALF + quad, 1)], ctr_v.at[pl.ds(13, 1)], in_sem.at[2])
+    fetch(ccp_h.at[pl.ds(duo, 1)], ccp_v.at[pl.ds(0, 1)], in_sem.at[3])
+    fetch(ccp_h.at[pl.ds(HALF + quad, 1)], ccp_v.at[pl.ds(1, 1)], in_sem.at[3])
     def fetch_near(at):
         def do():
             for k, (slots, leaves) in enumerate(near_kinds(at)):
@@ -334,7 +333,7 @@
 
     for at in range(2):
         when(core == at, fetch_near(at))
-    get_coupling = fetch(coupling_h, coupling_v, in_sem.at[10])
+    get_coupling = fetch(coupling_h, coupling_v, in_sem.at[8])
     own = ROWS
     for p in range(LEAVES // 2):
         matrices = basis_v[2 * p : 2 * p + 2].reshape(LANES, LANES)
@@ -437,8 +436,8 @@
             product = dot_nn(spread(chains[p], diagonal128), matrices).astype(BF16)
             reach_v[:, 2 * p * LANES : (2 * p + 1) * LANES] = product[:RANK]
             reach_v[:, (2 * p + 1) * LANES : (2 * p + 2) * LANES] = product[RANK:]
-        pltpu.make_async_copy(ctr_h.at[pl.ds(0, 14)], ctr_v, in_sem.at[8]).wait()
-        pltpu.make_async_copy(ccp_h.at[pl.ds(0, 2)], ccp_v, in_sem.at[9]).wait()
+        pltpu.make_async_copy(ctr_h.at[pl.ds(0, 14)], ctr_v, in_sem.at[2]).wait()
+        pltpu.make_async_copy(ccp_h.at[pl.ds(0, 2)], ccp_v, in_sem.at[3]).wait()
         for copy in get_coarse:
             copy.wait()
         for n in range(3):
@@ -534,7 +533,7 @@
 
     when(far_left, near_first)
     when(core == 0, far_gate)
-    when(core == 1, lambda: pl.semaphore_wait(far_ready, 1))
+    when(core == 1, lambda: pl.semaphore_wait(ready, 1))
     when(left_late, lambda: send_points(to_left))
     send_roots(False)
     when(left_late, lambda: send_pairs(to_left))
@@ -617,14 +616,22 @@
         return join(dot_nt(both(*picked).astype(BF16), matrices))
 
     fields = {14: couple(14)}
+
+    def sweep(parent, row, incoming):
+        matrices = transfer_v[row : row + 2].reshape(LANES, LANES)
+        down = dot_nn(spread(fields[parent], diagonal), matrices)
+        fields[row] = incoming[0] + down[:COLS]
+        fields[row + 1] = incoming[1] + down[COLS:]
+
+    ahead = None
     for first, width in ((12, 2), (8, 4), (0, 8)):
         for p in range(width // 2):
             row = first + 2 * p
-            matrices = transfer_v[row : row + 2].reshape(LANES, LANES)
-            incoming = [couple(row), couple(row + 1)]
-            down = dot_nn(spread(fields[first + width + p], diagonal), matrices)
-            fields[row] = incoming[0] + down[:COLS]
-            fields[row + 1] = incoming[1] + down[COLS:]
+            coupled = (first + width + p, row, [couple(row), couple(row + 1)])
+            if ahead is not None:
+                sweep(*ahead)
+            ahead = coupled
+    sweep(*ahead)
     for p in range(LEAVES // 2):
         matrices = basis_v[2 * p : 2 * p + 2].reshape(LANES, LANES)
         far = dot_nn(spread(fields[p], diagonal), matrices)
@@ -722,7 +729,7 @@
             pltpu.VMEM((LEAVES, COLS, LANES), F32),
             pltpu.VMEM((LEAVES, COLS, LANES), F32),
             pltpu.VMEM((LEAVES, COLS, LANES), F32),
-            dma((11,)),
+            dma((9,)),
             dma((2,)),
             dma((3,)),
             dma((3,)),
@@ -731,7 +738,6 @@
             dma,
             dma,
             dma,
-            pltpu.SemaphoreType.REGULAR,
             pltpu.SemaphoreType.REGULAR,
         ],
         compiler_params=pltpu.CompilerParams(

time: 16.1 us -> 16.4 us (1.019)
  the two profiles are of different devices: /device:TPU:7 before, /device:TPU:38 now
where the time goes in v7:
time: 16.4 us; the launch traced here: 16.3 us
  Pallas kernels  15.7 us (96%)
  local copies, waits for them, and re-layouts  0.63 us (4%)
    pallas_call x1, Pallas kernels, body(): pl.pallas_call(kernel, out_shape=pltpu.VMEM((COLS, LEAVES * LANES), F32),...  15.7 us
    unnamed x1, local copies, waits for them, and re-layouts  0.63 us

profile of v7, /device:TPU:38, one launch (start us, length us, event | category | flops | bytes accessed | tf_op | source)
XLA Modules:
  0.0 16.3 jit_solution(10409765751884903610)
XLA Ops:
  0.0 15.7 %shard_map.136 = f32[8,2048]{1,0:T(8,128)S(1)} custom-call(f32[8,2048]{1,0:T(8,128)} %rs_h.1, s32[16,128]{1,0:T(8,128)} %bitcast.5, bf16[16,64,128]{2,1,0:T(8,128)(2,1)} %basis_h.1, bf16[15,64,128]{2,1,0:T(8,128)(2,1)} %transfer_h.1, bf16[31,64,512]{2,1,0:T(8,128)(2,1)} %coupling_h.1, s32[8,31]{1,0:T(8,128)} %bitcast.6, s32[1,31]{1,0:T(1,128)} %bitcast.8, ...), custom_call_target="tpu_custom_call" | custom-call | tf_op jit(solution)/shard_map/pallas_call | solution.py:689
  15.7 0.6 %copy.16 = f32[8,2048]{1,0:T(8,128)} copy(f32[8,2048]{1,0:T(8,128)S(1)} %shard_map.136) | data formatting | bytes 131072
